TPU v7x, 32 devices: a whole 2x2x4 slice. The times are simulated.
32 devices in a mesh: parts: 2 (over y), clus: 4 (over z), mem: 2 (over x), sub: 2 (over core).
Axes of the slice: x: 2, y: 2, z: 4, core: 2. Of those that a mesh axis runs over, the one named last changes fastest.
Arguments:
- embeddings: bfloat16 [4096, 1024], P(('parts', 'clus', 'mem', 'sub')), parts along dimension 0, as said below
- labels: int32 [4096], P(('parts', 'clus', 'mem', 'sub')), parts along dimension 0, may hold values from 0 to 15, as said below
- member_rank: int32 [4096], P(('parts', 'clus', 'mem', 'sub')), parts along dimension 0, may hold values from 0 to 2047, each once
Outputs:
- nearest: float32 [4096], P(('parts', 'clus', 'mem', 'sub')), parts along dimension 0
There are 2 independent parts, one for each index of `parts`. A program takes and returns all parts, laid end to end along the dimension named above; each array names one. Nothing has to cross between parts.
Inputs may be any that keep to these rules, and one draw needn't show every extreme that they name: `embeddings`: each row has unit length up to rounding. Among the rows of one device, at most 32 have labels in any one group of 2 consecutive clusters (label // 2); on every device some group has exactly 32.
All inputs are finite; a program needn't handle non-finite values.
Results may differ from a plain program's by a relative error of at most 0.0003.
Values may be sent and summed in bfloat16 or wider, within the bound.
No kernel may reach another device: no remote copies, remote signals or barrier semaphores. Data moves between devices by JAX's collectives and lax.ppermute only.
A program may use at most 64 MiB of HBM per device.

v0:
```python
import jax
import jax.numpy as jnp
from jax import lax
from jax.experimental import pallas as pl
from jax.experimental.pallas import tpu as pltpu
from jax.sharding import PartitionSpec as P

LANES = 128
META_ROWS = 16
DIGIT = 256
VMEM_LIMIT = 24 * 1024 * 1024
NT = (((1,), (1,)), ((), ()))
NONE = -1.0


def meta_kernel(label_ref, rank_ref, meta_ref):
    kind = lax.broadcasted_iota(jnp.int32, meta_ref.shape, 0)
    rank = rank_ref[...]
    meta = jnp.where(kind == 0, label_ref[...], 0)
    meta = jnp.where(kind == 1, rank // DIGIT, meta)
    meta = jnp.where(kind == 2, rank % DIGIT, meta)
    meta_ref[...] = meta.astype(jnp.float32).astype(jnp.bfloat16)


def pack_kernel(meta_ref, chunks_ref, message_ref, sem):
    chunk_rows = chunks_ref.shape[0]
    copy = pltpu.make_async_copy(chunks_ref, message_ref.at[pl.ds(0, chunk_rows), :], sem)
    copy.start()
    message_ref[pl.ds(chunk_rows, META_ROWS), :] = meta_ref[...]
    copy.wait()


def rows_of(message):
    rows = message.shape[1]
    chunks = message.shape[0] // rows
    return jnp.concatenate([message[c * rows : (c + 1) * rows, :] for c in range(chunks)], axis=1)


def meta_of(message):
    meta = message[message.shape[0] - META_ROWS :, :].astype(jnp.float32)
    return meta[0:1], meta[1:2] * DIGIT + meta[2:3]


def best_kernel(line_count, back_count, mem_count, sub_count, *refs):
    plane_count = mem_count * sub_count
    plane = refs[:plane_count]
    lines = refs[plane_count : plane_count + line_count]
    outs = refs[line_count + plane_count :]
    plane_outs, back_outs = outs[:mem_count], outs[mem_count:]
    rows = lines[0].shape[1]

    line_rows = jnp.concatenate([rows_of(line) for line in lines], axis=0)
    columns = []
    for line in lines:
        label, rank = meta_of(line)
        columns.append(jnp.transpose(jnp.concatenate([label, rank] + [rank] * 6, axis=0)))
    columns = jnp.concatenate(columns, axis=0)
    line_label, line_rank = columns[:, 0:1], columns[:, 1:2]

    back = [None] * back_count
    for shift in range(mem_count):
        blocks = plane[shift * sub_count : (shift + 1) * sub_count]
        plane_rows = jnp.concatenate([rows_of(block) for block in blocks], axis=0)
        metas = [meta_of(block) for block in blocks]
        label = jnp.concatenate([meta[0] for meta in metas], axis=1)
        rank = jnp.concatenate([meta[1] for meta in metas], axis=1)
        scores = lax.dot_general(line_rows, plane_rows, NT, preferred_element_type=jnp.float32)
        scores = jnp.where(line_label == label, scores, NONE)
        forward = jnp.where(line_rank < rank, scores, NONE)
        best = jnp.max(forward, axis=0, keepdims=True)
        for turn in range(sub_count):
            plane_outs[shift][turn : turn + 1, :] = best[:, turn * rows : (turn + 1) * rows]
        for index in range(back_count):
            piece = slice((index + 1) * rows, (index + 2) * rows)
            backward = jnp.where(line_rank[piece] > rank, scores[piece], NONE)
            for turn in range(sub_count):
                part = backward[:, turn * rows : (turn + 1) * rows]
                back[index] = part if back[index] is None else jnp.maximum(back[index], part)
    for index in range(back_count):
        back_outs[index][...] = jnp.max(jnp.transpose(back[index]), axis=0, keepdims=True)


def body(embeddings, labels, member_rank):
    row_count, feature_count = embeddings.shape
    clus_count = lax.axis_size("clus")
    mem_count = lax.axis_size("mem")
    sub_count = lax.axis_size("sub")
    chunk_count = feature_count // LANES
    vmem = pl.BlockSpec(memory_space=pltpu.VMEM)
    params = pltpu.CompilerParams(vmem_limit_bytes=VMEM_LIMIT)

    def shifted(value, axis, order, distance):
        count = len(order)
        pairs = [(order[i], order[(i + distance) % count]) for i in range(count)]
        return lax.ppermute(value, axis, pairs)

    half = (clus_count + 1) // 2
    ring = [z for pair in zip(range(half), range(half, 2 * half)) for z in pair if z < clus_count]
    mem_order = list(range(mem_count))
    sub_order = list(range(sub_count))

    meta = pl.pallas_call(
        meta_kernel,
        out_shape=jax.ShapeDtypeStruct((META_ROWS, row_count), jnp.bfloat16),
        in_specs=[vmem, vmem],
        out_specs=vmem,
        compiler_params=params,
        name="meta",
    )(labels.reshape(1, row_count), member_rank.reshape(1, row_count))
    meta, rows = lax.optimization_barrier((meta, embeddings))
    chunks = rows.reshape(row_count, chunk_count, LANES).transpose(1, 0, 2)
    message = pl.pallas_call(
        pack_kernel,
        out_shape=jax.ShapeDtypeStruct((chunk_count * row_count + META_ROWS, LANES), jnp.bfloat16),
        in_specs=[vmem, pl.BlockSpec(memory_space=pl.ANY)],
        out_specs=vmem,
        scratch_shapes=[pltpu.SemaphoreType.DMA(())],
        compiler_params=params,
        name="pack",
    )(meta, chunks.reshape(chunk_count * row_count, LANES))

    distances = list(range(1, clus_count // 2 + 1))
    one_way = [d for d in distances if 2 * d != clus_count]
    lines = [message] + [shifted(message, "clus", ring, d) for d in distances]
    plane = []
    for shift in range(mem_count):
        block = shifted(message, "mem", mem_order, shift) if shift else message
        plane.append(block)
        plane.extend(shifted(block, "sub", sub_order, turn) for turn in range(1, sub_count))

    outs = pl.pallas_call(
        lambda *refs: best_kernel(len(lines), len(one_way), mem_count, sub_count, *refs),
        out_shape=[jax.ShapeDtypeStruct((sub_count, row_count), jnp.float32)] * mem_count
        + [jax.ShapeDtypeStruct((1, row_count), jnp.float32)] * len(one_way),
        in_specs=[vmem] * (len(lines) + len(plane)),
        out_specs=[vmem] * (mem_count + len(one_way)),
        compiler_params=params,
        name="best",
    )(*plane, *lines)
    table = outs[0]
    for shift in range(1, mem_count):
        table = jnp.maximum(table, shifted(outs[shift], "mem", mem_order, -shift))
    nearest = table[0:1]
    for turn in range(1, sub_count):
        part = shifted(table[turn : turn + 1], "sub", sub_order, -turn)
        nearest = jnp.maximum(nearest, part)
    for distance, value in zip(one_way, outs[mem_count:]):
        nearest = jnp.maximum(nearest, shifted(value, "clus", ring, -distance))
    return nearest.reshape(row_count)


def solution(mesh):
    placed = (
        P(("parts", "clus", "mem", "sub"), None),
        P(("parts", "clus", "mem", "sub")),
        P(("parts", "clus", "mem", "sub")),
    )
    return jax.shard_map(
        body,
        mesh=mesh,
        in_specs=placed,
        out_specs=P(("parts", "clus", "mem", "sub")),
        check_vma=False,
    )
```

profile of v0, /device:TPU:0, one launch (start us, length us, event | category | flops | bytes accessed | tf_op | source)
XLA Modules:
  0.0 26.1 jit_solution(16258186294669846596)
XLA Ops:
  0.0 0.0 copy-start
  0.0 0.0 copy-start.1
  0.0 0.0 copy-start.2
  0.0 0.7 %copy-done.1 = s32[128]{0:T(128)S(1)} copy-done((s32[128]{0:T(128)S(1)}, s32[128]{0:T(128)}, u32[]{:S(2)}) %copy-start.1) | copy-done | bytes 536
  0.7 0.0 copy-done.2
  0.7 0.3 copy-done
  1.1 3.0 %collective-permute-start.1 = (bf16[1040,128]{1,0:T(8,128)(2,1)S(1)}, bf16[1040,128]{1,0:T(8,128)(2,1)S(1)}, u32[]{:S(2)}, u32[]{:S(2)}) collective-permute-start(bf16[1040,128]{1,0:T(8,128)(2,1)S(1)} %pack.1.refs_0_.refs_4_), channel_id=1, source_target_pairs={{0,2},{2,0},{1,3},{3,1},{4,6},{6,4},{5,7},{7,5},{8,10},{10,8},{9,1... | collective-permute-start | bytes 798728 | tf_op jit(solution)/shard_map/ppermute | solution.py:95
  4.1 1.6 %collective-permute-start.4 = (bf16[1040,128]{1,0:T(8,128)(2,1)S(1)}, bf16[1040,128]{1,0:T(8,128)(2,1)S(1)}, u32[]{:S(2)}, u32[]{:S(2)}) collective-permute-start(bf16[1040,128]{1,0:T(8,128)(2,1)S(1)} %pack.1.refs_0_.refs_4_), channel_id=1, source_target_pairs={{0,4},{8,12},{4,0},{12,8},{1,5},{9,13},{5,1},{13,9},{2,6},{10,14},... | collective-permute-start | bytes 798728 | tf_op jit(solution)/shard_map/ppermute | solution.py:95
  5.7 2.6 %collective-permute-start.3 = (bf16[1040,128]{1,0:T(8,128)(2,1)S(1)}, bf16[1040,128]{1,0:T(8,128)(2,1)S(1)}, u32[]{:S(2)}, u32[]{:S(2)}) collective-permute-start(bf16[1040,128]{1,0:T(8,128)(2,1)S(1)} %pack.1.refs_0_.refs_4_), channel_id=1, source_target_pairs={{0,8},{8,4},{4,12},{12,0},{1,9},{9,5},{5,13},{13,1},{2,10},{10,6},... | collective-permute-start | bytes 798728 | tf_op jit(solution)/shard_map/ppermute | solution.py:95
  8.2 0.0 collective-permute-start
  8.2 2.2 %collective-permute-done.1.refs_2_ = bf16[1040,128]{1,0:T(8,128)(2,1)S(1)} collective-permute-done((bf16[1040,128]{1,0:T(8,128)(2,1)S(1)}, bf16[1040,128]{1,0:T(8,128)(2,1)S(1)}, u32[]{:S(2)}, u32[]{:S(2)}) %collective-permute-start.1) | collective-permute-done | bytes 266272 | tf_op jit(solution)/shard_map/ppermute | solution.py:95
  10.5 0.0 collective-permute-start.2
  10.5 2.0 %collective-permute-done.4.refs_6_ = bf16[1040,128]{1,0:T(8,128)(2,1)S(1)} collective-permute-done((bf16[1040,128]{1,0:T(8,128)(2,1)S(1)}, bf16[1040,128]{1,0:T(8,128)(2,1)S(1)}, u32[]{:S(2)}, u32[]{:S(2)}) %collective-permute-start.4) | collective-permute-done | bytes 266272 | tf_op jit(solution)/shard_map/ppermute | solution.py:95
  12.5 7.3 %collective-permute-done.3.refs_5_ = bf16[1040,128]{1,0:T(8,128)(2,1)S(1)} collective-permute-done((bf16[1040,128]{1,0:T(8,128)(2,1)S(1)}, bf16[1040,128]{1,0:T(8,128)(2,1)S(1)}, u32[]{:S(2)}, u32[]{:S(2)}) %collective-permute-start.3) | collective-permute-done | bytes 266272 | tf_op jit(solution)/shard_map/ppermute | solution.py:95
  19.8 0.0 collective-permute-done.refs_1_
  19.8 0.0 collective-permute-done.2.refs_3_
  19.8 0.7 %best.1 = (f32[2,128]{1,0:T(2,128)S(1)}, f32[2,128]{1,0:T(2,128)S(1)}, f32[1,128]{1,0:T(1,128)S(1)}) custom-call(bf16[1040,128]{1,0:T(8,128)(2,1)S(1)} %pack.1.refs_0_.refs_4_, bf16[1040,128]{1,0:T(8,128)(2,1)S(1)} %collective-permute-done.refs_1_, bf16[1040,128]{1,0:T(8,128)(2,1)S(1)} %collective-permute-done.1.refs_2_, ...), custom_call_target="tpu_custom_call" | custom-call | tf_op jit(solution)/shard_map/best/pallas_call | solution.py:131
  20.5 0.6 %collective-permute-start.5 = (f32[2,128]{1,0:T(2,128)S(1)}, f32[2,128]{1,0:T(2,128)S(1)}, u32[]{:S(2)}, u32[]{:S(2)}) collective-permute-start(f32[2,128]{1,0:T(2,128)S(1)} %get-tuple-element.13), channel_id=1, source_target_pairs={{0,2},{2,0},{1,3},{3,1},{4,6},{6,4},{5,7},{7,5},{8,10},{10,8},{9,1... | collective-permute-start | bytes 3080 | tf_op jit(solution)/shard_map/ppermute | solution.py:95
  21.1 2.6 %collective-permute-start.7 = (f32[1,128]{1,0:T(1,128)S(1)}, f32[1,128]{1,0:T(1,128)S(1)}, u32[]{:S(2)}, u32[]{:S(2)}) collective-permute-start(f32[1,128]{1,0:T(1,128)S(1)} %get-tuple-element.14), channel_id=1, source_target_pairs={{0,12},{8,0},{4,8},{12,4},{1,13},{9,1},{5,9},{13,5},{2,14},{10,2},... | collective-permute-start | bytes 1544 | tf_op jit(solution)/shard_map/ppermute | solution.py:95
  23.7 0.4 %collective-permute-done.5 = f32[2,128]{1,0:T(2,128)S(1)} collective-permute-done((f32[2,128]{1,0:T(2,128)S(1)}, f32[2,128]{1,0:T(2,128)S(1)}, u32[]{:S(2)}, u32[]{:S(2)}) %collective-permute-start.5) | collective-permute-done | bytes 1056 | tf_op jit(solution)/shard_map/ppermute | solution.py:95
  24.1 0.0 collective-permute-start.6
  24.2 1.4 %collective-permute-done.7 = f32[1,128]{1,0:T(1,128)S(1)} collective-permute-done((f32[1,128]{1,0:T(1,128)S(1)}, f32[1,128]{1,0:T(1,128)S(1)}, u32[]{:S(2)}, u32[]{:S(2)}) %collective-permute-start.7) | collective-permute-done | bytes 544 | tf_op jit(solution)/shard_map/ppermute | solution.py:95
  25.5 0.0 collective-permute-done.6
  25.5 0.5 %maximum_bitcast_fusion = f32[128]{0:T(128)} fusion(f32[1,128]{1,0:T(1,128)S(1)} %collective-permute-done.7, f32[1,128]{1,0:T(1,128)S(1)} %collective-permute-done.6, f32[2,128]{1,0:T(2,128)S(1)} %max.9), kind=kLoop, calls=%fused_computation.1 | loop fusion | flops 256 | bytes 2048 | tf_op jit(solution)/shard_map/reshape | solution.py:149
  (5 shorter events, 0.1 us)
Async XLA Ops:
  0.0 1.0 %copy-start = (bf16[128,1024]{1,0:T(8,128)(2,1)S(1)}, bf16[128,1024]{1,0:T(8,128)(2,1)}, u32[]{:S(2)}) copy-start(bf16[128,1024]{1,0:T(8,128)(2,1)} %param.3) | copy-start | bytes 786436
  0.0 0.7 %copy-start.1 = (s32[128]{0:T(128)S(1)}, s32[128]{0:T(128)}, u32[]{:S(2)}) copy-start(s32[128]{0:T(128)} %param.4) | copy-start | bytes 1540
  0.0 0.7 %copy-start.2 = (s32[128]{0:T(128)S(1)}, s32[128]{0:T(128)}, u32[]{:S(2)}) copy-start(s32[128]{0:T(128)} %param.5) | copy-start | bytes 1540
  1.1 9.4 %collective-permute-start.1 = (bf16[1040,128]{1,0:T(8,128)(2,1)S(1)}, bf16[1040,128]{1,0:T(8,128)(2,1)S(1)}, u32[]{:S(2)}, u32[]{:S(2)}) collective-permute-start(bf16[1040,128]{1,0:T(8,128)(2,1)S(1)} %pack.1.refs_0_.refs_4_), channel_id=1, source_target_pairs={{0,2},{2,0},{1,3},{3,1},{4,6},{6,4},{5,7},{7,5},{8,10},{10,8},{9,1... | collective-permute-start | bytes 798728 | tf_op jit(solution)/shard_map/ppermute | solution.py:95
  4.1 8.4 %collective-permute-start.4 = (bf16[1040,128]{1,0:T(8,128)(2,1)S(1)}, bf16[1040,128]{1,0:T(8,128)(2,1)S(1)}, u32[]{:S(2)}, u32[]{:S(2)}) collective-permute-start(bf16[1040,128]{1,0:T(8,128)(2,1)S(1)} %pack.1.refs_0_.refs_4_), channel_id=1, source_target_pairs={{0,4},{8,12},{4,0},{12,8},{1,5},{9,13},{5,1},{13,9},{2,6},{10,14},... | collective-permute-start | bytes 798728 | tf_op jit(solution)/shard_map/ppermute | solution.py:95
  5.7 14.1 %collective-permute-start.3 = (bf16[1040,128]{1,0:T(8,128)(2,1)S(1)}, bf16[1040,128]{1,0:T(8,128)(2,1)S(1)}, u32[]{:S(2)}, u32[]{:S(2)}) collective-permute-start(bf16[1040,128]{1,0:T(8,128)(2,1)S(1)} %pack.1.refs_0_.refs_4_), channel_id=1, source_target_pairs={{0,8},{8,4},{4,12},{12,0},{1,9},{9,5},{5,13},{13,1},{2,10},{10,6},... | collective-permute-start | bytes 798728 | tf_op jit(solution)/shard_map/ppermute | solution.py:95
  8.2 11.5 %collective-permute-start = (bf16[1040,128]{1,0:T(8,128)(2,1)S(1)}, bf16[1040,128]{1,0:T(8,128)(2,1)S(1)}, u32[]{:S(2)}, u32[]{:S(2)}) collective-permute-start(bf16[1040,128]{1,0:T(8,128)(2,1)S(1)} %pack.1.refs_0_.refs_4_), channel_id=1, source_target_pairs={{0,1},{1,0},{2,3},{3,2},{4,5},{5,4},{6,7},{7,6},{8,9},{9,8},{10,11... | collective-permute-start | bytes 798728 | tf_op jit(solution)/shard_map/ppermute | solution.py:95
  10.5 9.3 %collective-permute-start.2 = (bf16[1040,128]{1,0:T(8,128)(2,1)S(1)}, bf16[1040,128]{1,0:T(8,128)(2,1)S(1)}, u32[]{:S(2)}, u32[]{:S(2)}) collective-permute-start(bf16[1040,128]{1,0:T(8,128)(2,1)S(1)} %collective-permute-done.1.refs_2_), channel_id=1, source_target_pairs={{0,1},{1,0},{2,3},{3,2},{4,5},{5,4},{6,7},{7,6},{8,9},{9,8},{10,11... | collective-permute-start | bytes 798728 | tf_op jit(solution)/shard_map/ppermute | solution.py:95
  20.5 3.6 %collective-permute-start.5 = (f32[2,128]{1,0:T(2,128)S(1)}, f32[2,128]{1,0:T(2,128)S(1)}, u32[]{:S(2)}, u32[]{:S(2)}) collective-permute-start(f32[2,128]{1,0:T(2,128)S(1)} %get-tuple-element.13), channel_id=1, source_target_pairs={{0,2},{2,0},{1,3},{3,1},{4,6},{6,4},{5,7},{7,5},{8,10},{10,8},{9,1... | collective-permute-start | bytes 3080 | tf_op jit(solution)/shard_map/ppermute | solution.py:95
  21.1 4.4 %collective-permute-start.7 = (f32[1,128]{1,0:T(1,128)S(1)}, f32[1,128]{1,0:T(1,128)S(1)}, u32[]{:S(2)}, u32[]{:S(2)}) collective-permute-start(f32[1,128]{1,0:T(1,128)S(1)} %get-tuple-element.14), channel_id=1, source_target_pairs={{0,12},{8,0},{4,8},{12,4},{1,13},{9,1},{5,9},{13,5},{2,14},{10,2},... | collective-permute-start | bytes 1544 | tf_op jit(solution)/shard_map/ppermute | solution.py:95
  24.1 1.4 %collective-permute-start.6 = (f32[1,128]{1,0:T(1,128)S(1)}, f32[1,128]{1,0:T(1,128)S(1)}, u32[]{:S(2)}, u32[]{:S(2)}) collective-permute-start(f32[1,128]{1,0:T(1,128)S(1)} %slice.7), channel_id=1, source_target_pairs={{0,1},{1,0},{2,3},{3,2},{4,5},{5,4},{6,7},{7,6},{8,9},{9,8},{10,11... | collective-permute-start | bytes 1544 | tf_op jit(solution)/shard_map/ppermute | solution.py:95
where the time goes:
time: 26.2 us; the launch traced here: 26.1 us
  waiting for transfers between devices  13.4 us (51%)
  starting transfers between devices  10.4 us (40%)
  local copies, waits for them, and re-layouts  1.02 us (4%)
  Pallas kernels  0.77 us (3%)
  other arithmetic  0.52 us (2%)
    ppermute x8, waiting for transfers between devices, shifted(): return lax.ppermute(value, axis, pairs)  13.4 us
    ppermute x8, starting transfers between devices, shifted(): return lax.ppermute(value, axis, pairs)  10.4 us
    unnamed x6, local copies, waits for them, and re-layouts  0.97 us
    pallas_call x1, Pallas kernels, body(): pl.pallas_call(lambda *refs: best_kernel(len(lines), len(one_way), mem_co...  0.73 us
  transfers between devices with their start and end apart: 8, of which 5 were waited for; matrix products, arithmetic and copies ran while one was open for 0% of the time, Pallas kernels for 0%

commit v1 on v0

--- a/solution.py
+++ b/solution.py
@@ -6,6 +6,7 @@
 from jax.sharding import PartitionSpec as P
 
 LANES = 128
+SUBLANES = 8
 META_ROWS = 16
 DIGIT = 256
 VMEM_LIMIT = 24 * 1024 * 1024
@@ -50,34 +51,33 @@
     rows = lines[0].shape[1]
 
     line_rows = jnp.concatenate([rows_of(line) for line in lines], axis=0)
-    columns = []
-    for line in lines:
-        label, rank = meta_of(line)
-        columns.append(jnp.transpose(jnp.concatenate([label, rank] + [rank] * 6, axis=0)))
-    columns = jnp.concatenate(columns, axis=0)
-    line_label, line_rank = columns[:, 0:1], columns[:, 1:2]
+    plane_rows = jnp.concatenate([rows_of(block) for block in plane], axis=0)
+    metas = [part for line in lines for part in meta_of(line)]
+    metas += [metas[-1]] * (-len(metas) % SUBLANES)
+    columns = jnp.transpose(jnp.concatenate(metas, axis=0))
+    line_label, line_rank = [
+        jnp.concatenate(
+            [columns[:, 2 * index + part : 2 * index + part + 1] for index in range(line_count)],
+            axis=0,
+        )
+        for part in range(2)
+    ]
+    label, rank = [jnp.concatenate(parts, axis=1) for parts in zip(*map(meta_of, plane))]
 
-    back = [None] * back_count
-    for shift in range(mem_count):
-        blocks = plane[shift * sub_count : (shift + 1) * sub_count]
-        plane_rows = jnp.concatenate([rows_of(block) for block in blocks], axis=0)
-        metas = [meta_of(block) for block in blocks]
-        label = jnp.concatenate([meta[0] for meta in metas], axis=1)
-        rank = jnp.concatenate([meta[1] for meta in metas], axis=1)
-        scores = lax.dot_general(line_rows, plane_rows, NT, preferred_element_type=jnp.float32)
-        scores = jnp.where(line_label == label, scores, NONE)
-        forward = jnp.where(line_rank < rank, scores, NONE)
-        best = jnp.max(forward, axis=0, keepdims=True)
-        for turn in range(sub_count):
-            plane_outs[shift][turn : turn + 1, :] = best[:, turn * rows : (turn + 1) * rows]
-        for index in range(back_count):
-            piece = slice((index + 1) * rows, (index + 2) * rows)
-            backward = jnp.where(line_rank[piece] > rank, scores[piece], NONE)
-            for turn in range(sub_count):
-                part = backward[:, turn * rows : (turn + 1) * rows]
-                back[index] = part if back[index] is None else jnp.maximum(back[index], part)
+    scores = lax.dot_general(line_rows, plane_rows, NT, preferred_element_type=jnp.float32)
+    scores = jnp.where(line_label == label, scores, NONE)
+    forward = jnp.where(line_rank < rank, scores, NONE)
+    best = jnp.max(forward, axis=0, keepdims=True)
+    for block in range(plane_count):
+        shift, turn = block // sub_count, block % sub_count
+        plane_outs[shift][turn : turn + 1, :] = best[:, block * rows : (block + 1) * rows]
     for index in range(back_count):
-        back_outs[index][...] = jnp.max(jnp.transpose(back[index]), axis=0, keepdims=True)
+        piece = slice((index + 1) * rows, (index + 2) * rows)
+        backward = jnp.where(line_rank[piece] > rank, scores[piece], NONE)
+        back = backward[:, :rows]
+        for block in range(1, plane_count):
+            back = jnp.maximum(back, backward[:, block * rows : (block + 1) * rows])
+        back_outs[index][...] = jnp.max(jnp.transpose(back), axis=0, keepdims=True)
 
 
 def body(embeddings, labels, member_rank):

time: 26.2 us -> 26.2 us (level)
  no operation moved by 1% of the time
where the time goes in v1:
time: 26.2 us; the launch traced here: 26 us
  waiting for transfers between devices  13.4 us (51%)
  starting transfers between devices  10.4 us (40%)
  local copies, waits for them, and re-layouts  1.02 us (4%)
  Pallas kernels  0.75 us (3%)
  other arithmetic  0.52 us (2%)
    ppermute x8, waiting for transfers between devices, shifted(): return lax.ppermute(value, axis, pairs)  13.4 us
    ppermute x8, starting transfers between devices, shifted(): return lax.ppermute(value, axis, pairs)  10.4 us
    unnamed x6, local copies, waits for them, and re-layouts  0.97 us
    pallas_call x1, Pallas kernels, body(): pl.pallas_call(lambda *refs: best_kernel(len(lines), len(one_way), mem_co...  0.7 us
  transfers between devices with their start and end apart: 8, of which 5 were waited for; matrix products, arithmetic and copies ran while one was open for 0% of the time, Pallas kernels for 0%

profile of v1, /device:TPU:0, one launch (start us, length us, event | category | flops | bytes accessed | tf_op | source)
XLA Modules:
  0.0 26.0 jit_solution(13040983360557386350)
XLA Ops:
  0.0 0.0 copy-start
  0.0 0.0 copy-start.1
  0.0 0.0 copy-start.2
  0.0 0.7 %copy-done.1 = s32[128]{0:T(128)S(1)} copy-done((s32[128]{0:T(128)S(1)}, s32[128]{0:T(128)}, u32[]{:S(2)}) %copy-start.1) | copy-done | bytes 536
  0.7 0.0 copy-done.2
  0.7 0.3 copy-done
  1.1 3.0 %collective-permute-start.1 = (bf16[1040,128]{1,0:T(8,128)(2,1)S(1)}, bf16[1040,128]{1,0:T(8,128)(2,1)S(1)}, u32[]{:S(2)}, u32[]{:S(2)}) collective-permute-start(bf16[1040,128]{1,0:T(8,128)(2,1)S(1)} %pack.1.refs_0_.refs_4_), channel_id=1, source_target_pairs={{0,2},{2,0},{1,3},{3,1},{4,6},{6,4},{5,7},{7,5},{8,10},{10,8},{9,1... | collective-permute-start | bytes 798728 | tf_op jit(solution)/shard_map/ppermute | solution.py:95
  4.1 1.6 %collective-permute-start.4 = (bf16[1040,128]{1,0:T(8,128)(2,1)S(1)}, bf16[1040,128]{1,0:T(8,128)(2,1)S(1)}, u32[]{:S(2)}, u32[]{:S(2)}) collective-permute-start(bf16[1040,128]{1,0:T(8,128)(2,1)S(1)} %pack.1.refs_0_.refs_4_), channel_id=1, source_target_pairs={{0,4},{8,12},{4,0},{12,8},{1,5},{9,13},{5,1},{13,9},{2,6},{10,14},... | collective-permute-start | bytes 798728 | tf_op jit(solution)/shard_map/ppermute | solution.py:95
  5.7 2.6 %collective-permute-start.3 = (bf16[1040,128]{1,0:T(8,128)(2,1)S(1)}, bf16[1040,128]{1,0:T(8,128)(2,1)S(1)}, u32[]{:S(2)}, u32[]{:S(2)}) collective-permute-start(bf16[1040,128]{1,0:T(8,128)(2,1)S(1)} %pack.1.refs_0_.refs_4_), channel_id=1, source_target_pairs={{0,8},{8,4},{4,12},{12,0},{1,9},{9,5},{5,13},{13,1},{2,10},{10,6},... | collective-permute-start | bytes 798728 | tf_op jit(solution)/shard_map/ppermute | solution.py:95
  8.2 0.0 collective-permute-start
  8.2 2.2 %collective-permute-done.1.refs_2_ = bf16[1040,128]{1,0:T(8,128)(2,1)S(1)} collective-permute-done((bf16[1040,128]{1,0:T(8,128)(2,1)S(1)}, bf16[1040,128]{1,0:T(8,128)(2,1)S(1)}, u32[]{:S(2)}, u32[]{:S(2)}) %collective-permute-start.1) | collective-permute-done | bytes 266272 | tf_op jit(solution)/shard_map/ppermute | solution.py:95
  10.5 0.0 collective-permute-start.2
  10.5 2.0 %collective-permute-done.4.refs_6_ = bf16[1040,128]{1,0:T(8,128)(2,1)S(1)} collective-permute-done((bf16[1040,128]{1,0:T(8,128)(2,1)S(1)}, bf16[1040,128]{1,0:T(8,128)(2,1)S(1)}, u32[]{:S(2)}, u32[]{:S(2)}) %collective-permute-start.4) | collective-permute-done | bytes 266272 | tf_op jit(solution)/shard_map/ppermute | solution.py:95
  12.5 7.3 %collective-permute-done.3.refs_5_ = bf16[1040,128]{1,0:T(8,128)(2,1)S(1)} collective-permute-done((bf16[1040,128]{1,0:T(8,128)(2,1)S(1)}, bf16[1040,128]{1,0:T(8,128)(2,1)S(1)}, u32[]{:S(2)}, u32[]{:S(2)}) %collective-permute-start.3) | collective-permute-done | bytes 266272 | tf_op jit(solution)/shard_map/ppermute | solution.py:95
  19.8 0.0 collective-permute-done.refs_1_
  19.8 0.0 collective-permute-done.2.refs_3_
  19.8 0.7 %best.1 = (f32[2,128]{1,0:T(2,128)S(1)}, f32[2,128]{1,0:T(2,128)S(1)}, f32[1,128]{1,0:T(1,128)S(1)}) custom-call(bf16[1040,128]{1,0:T(8,128)(2,1)S(1)} %pack.1.refs_0_.refs_4_, bf16[1040,128]{1,0:T(8,128)(2,1)S(1)} %collective-permute-done.refs_1_, bf16[1040,128]{1,0:T(8,128)(2,1)S(1)} %collective-permute-done.1.refs_2_, ...), custom_call_target="tpu_custom_call" | custom-call | tf_op jit(solution)/shard_map/best/pallas_call | solution.py:131
  20.5 0.6 %collective-permute-start.5 = (f32[2,128]{1,0:T(2,128)S(1)}, f32[2,128]{1,0:T(2,128)S(1)}, u32[]{:S(2)}, u32[]{:S(2)}) collective-permute-start(f32[2,128]{1,0:T(2,128)S(1)} %get-tuple-element.13), channel_id=1, source_target_pairs={{0,2},{2,0},{1,3},{3,1},{4,6},{6,4},{5,7},{7,5},{8,10},{10,8},{9,1... | collective-permute-start | bytes 3080 | tf_op jit(solution)/shard_map/ppermute | solution.py:95
  21.1 2.6 %collective-permute-start.7 = (f32[1,128]{1,0:T(1,128)S(1)}, f32[1,128]{1,0:T(1,128)S(1)}, u32[]{:S(2)}, u32[]{:S(2)}) collective-permute-start(f32[1,128]{1,0:T(1,128)S(1)} %get-tuple-element.14), channel_id=1, source_target_pairs={{0,12},{8,0},{4,8},{12,4},{1,13},{9,1},{5,9},{13,5},{2,14},{10,2},... | collective-permute-start | bytes 1544 | tf_op jit(solution)/shard_map/ppermute | solution.py:95
  23.7 0.5 %collective-permute-done.5 = f32[2,128]{1,0:T(2,128)S(1)} collective-permute-done((f32[2,128]{1,0:T(2,128)S(1)}, f32[2,128]{1,0:T(2,128)S(1)}, u32[]{:S(2)}, u32[]{:S(2)}) %collective-permute-start.5) | collective-permute-done | bytes 1056 | tf_op jit(solution)/shard_map/ppermute | solution.py:95
  24.1 0.0 collective-permute-start.6
  24.1 1.4 %collective-permute-done.7 = f32[1,128]{1,0:T(1,128)S(1)} collective-permute-done((f32[1,128]{1,0:T(1,128)S(1)}, f32[1,128]{1,0:T(1,128)S(1)}, u32[]{:S(2)}, u32[]{:S(2)}) %collective-permute-start.7) | collective-permute-done | bytes 544 | tf_op jit(solution)/shard_map/ppermute | solution.py:95
  25.5 0.0 collective-permute-done.6
  25.5 0.5 %maximum_bitcast_fusion = f32[128]{0:T(128)} fusion(f32[1,128]{1,0:T(1,128)S(1)} %collective-permute-done.7, f32[1,128]{1,0:T(1,128)S(1)} %collective-permute-done.6, f32[2,128]{1,0:T(2,128)S(1)} %max.9), kind=kLoop, calls=%fused_computation.1 | loop fusion | flops 256 | bytes 2048 | tf_op jit(solution)/shard_map/reshape | solution.py:149
  (5 shorter events, 0.1 us)
Async XLA Ops:
  0.0 1.0 %copy-start = (bf16[128,1024]{1,0:T(8,128)(2,1)S(1)}, bf16[128,1024]{1,0:T(8,128)(2,1)}, u32[]{:S(2)}) copy-start(bf16[128,1024]{1,0:T(8,128)(2,1)} %param.3) | copy-start | bytes 786436
  0.0 0.7 %copy-start.1 = (s32[128]{0:T(128)S(1)}, s32[128]{0:T(128)}, u32[]{:S(2)}) copy-start(s32[128]{0:T(128)} %param.4) | copy-start | bytes 1540
  0.0 0.7 %copy-start.2 = (s32[128]{0:T(128)S(1)}, s32[128]{0:T(128)}, u32[]{:S(2)}) copy-start(s32[128]{0:T(128)} %param.5) | copy-start | bytes 1540
  1.1 9.4 %collective-permute-start.1 = (bf16[1040,128]{1,0:T(8,128)(2,1)S(1)}, bf16[1040,128]{1,0:T(8,128)(2,1)S(1)}, u32[]{:S(2)}, u32[]{:S(2)}) collective-permute-start(bf16[1040,128]{1,0:T(8,128)(2,1)S(1)} %pack.1.refs_0_.refs_4_), channel_id=1, source_target_pairs={{0,2},{2,0},{1,3},{3,1},{4,6},{6,4},{5,7},{7,5},{8,10},{10,8},{9,1... | collective-permute-start | bytes 798728 | tf_op jit(solution)/shard_map/ppermute | solution.py:95
  4.1 8.4 %collective-permute-start.4 = (bf16[1040,128]{1,0:T(8,128)(2,1)S(1)}, bf16[1040,128]{1,0:T(8,128)(2,1)S(1)}, u32[]{:S(2)}, u32[]{:S(2)}) collective-permute-start(bf16[1040,128]{1,0:T(8,128)(2,1)S(1)} %pack.1.refs_0_.refs_4_), channel_id=1, source_target_pairs={{0,4},{8,12},{4,0},{12,8},{1,5},{9,13},{5,1},{13,9},{2,6},{10,14},... | collective-permute-start | bytes 798728 | tf_op jit(solution)/shard_map/ppermute | solution.py:95
  5.7 14.1 %collective-permute-start.3 = (bf16[1040,128]{1,0:T(8,128)(2,1)S(1)}, bf16[1040,128]{1,0:T(8,128)(2,1)S(1)}, u32[]{:S(2)}, u32[]{:S(2)}) collective-permute-start(bf16[1040,128]{1,0:T(8,128)(2,1)S(1)} %pack.1.refs_0_.refs_4_), channel_id=1, source_target_pairs={{0,8},{8,4},{4,12},{12,0},{1,9},{9,5},{5,13},{13,1},{2,10},{10,6},... | collective-permute-start | bytes 798728 | tf_op jit(solution)/shard_map/ppermute | solution.py:95
  8.2 11.5 %collective-permute-start = (bf16[1040,128]{1,0:T(8,128)(2,1)S(1)}, bf16[1040,128]{1,0:T(8,128)(2,1)S(1)}, u32[]{:S(2)}, u32[]{:S(2)}) collective-permute-start(bf16[1040,128]{1,0:T(8,128)(2,1)S(1)} %pack.1.refs_0_.refs_4_), channel_id=1, source_target_pairs={{0,1},{1,0},{2,3},{3,2},{4,5},{5,4},{6,7},{7,6},{8,9},{9,8},{10,11... | collective-permute-start | bytes 798728 | tf_op jit(solution)/shard_map/ppermute | solution.py:95
  10.5 9.3 %collective-permute-start.2 = (bf16[1040,128]{1,0:T(8,128)(2,1)S(1)}, bf16[1040,128]{1,0:T(8,128)(2,1)S(1)}, u32[]{:S(2)}, u32[]{:S(2)}) collective-permute-start(bf16[1040,128]{1,0:T(8,128)(2,1)S(1)} %collective-permute-done.1.refs_2_), channel_id=1, source_target_pairs={{0,1},{1,0},{2,3},{3,2},{4,5},{5,4},{6,7},{7,6},{8,9},{9,8},{10,11... | collective-permute-start | bytes 798728 | tf_op jit(solution)/shard_map/ppermute | solution.py:95
  20.5 3.6 %collective-permute-start.5 = (f32[2,128]{1,0:T(2,128)S(1)}, f32[2,128]{1,0:T(2,128)S(1)}, u32[]{:S(2)}, u32[]{:S(2)}) collective-permute-start(f32[2,128]{1,0:T(2,128)S(1)} %get-tuple-element.13), channel_id=1, source_target_pairs={{0,2},{2,0},{1,3},{3,1},{4,6},{6,4},{5,7},{7,5},{8,10},{10,8},{9,1... | collective-permute-start | bytes 3080 | tf_op jit(solution)/shard_map/ppermute | solution.py:95
  21.1 4.4 %collective-permute-start.7 = (f32[1,128]{1,0:T(1,128)S(1)}, f32[1,128]{1,0:T(1,128)S(1)}, u32[]{:S(2)}, u32[]{:S(2)}) collective-permute-start(f32[1,128]{1,0:T(1,128)S(1)} %get-tuple-element.14), channel_id=1, source_target_pairs={{0,12},{8,0},{4,8},{12,4},{1,13},{9,1},{5,9},{13,5},{2,14},{10,2},... | collective-permute-start | bytes 1544 | tf_op jit(solution)/shard_map/ppermute | solution.py:95
  24.1 1.4 %collective-permute-start.6 = (f32[1,128]{1,0:T(1,128)S(1)}, f32[1,128]{1,0:T(1,128)S(1)}, u32[]{:S(2)}, u32[]{:S(2)}) collective-permute-start(f32[1,128]{1,0:T(1,128)S(1)} %slice.7), channel_id=1, source_target_pairs={{0,1},{1,0},{2,3},{3,2},{4,5},{5,4},{6,7},{7,6},{8,9},{9,8},{10,11... | collective-permute-start | bytes 1544 | tf_op jit(solution)/shard_map/ppermute | solution.py:95

commit v2 on v1

--- a/solution.py
+++ b/solution.py
@@ -122,9 +122,11 @@
     distances = list(range(1, clus_count // 2 + 1))
     one_way = [d for d in distances if 2 * d != clus_count]
     lines = [message] + [shifted(message, "clus", ring, d) for d in distances]
+    neighbours = [shifted(message, "mem", mem_order, shift) for shift in range(1, mem_count)]
+    neighbours, arrived = lax.optimization_barrier((neighbours, lines[1 + len(one_way) :]))
+    lines[1 + len(one_way) :] = arrived
     plane = []
-    for shift in range(mem_count):
-        block = shifted(message, "mem", mem_order, shift) if shift else message
+    for block in [message] + neighbours:
         plane.append(block)
         plane.extend(shifted(block, "sub", sub_order, turn) for turn in range(1, sub_count))
 

time: 26.2 us -> 25.9 us (0.989)
  waiting for transfers between devices: 13.4 us -> 11.8 us
  starting transfers between devices: 10.4 us -> 11.6 us
    ppermute x8, waiting for transfers between devices: 13.4 us -> 11.8 us  [shifted(): return lax.ppermute(value, axis, pairs)]
    ppermute x8, starting transfers between devices: 10.4 us -> 11.6 us  [shifted(): return lax.ppermute(value, axis, pairs)]
  transfers between devices with their start and end apart: 8 -> 8, of which waited for: 5 -> 4; matrix products, arithmetic and copies ran while one was open for 0% -> 0% of each run, Pallas kernels for 0% -> 0%
where the time goes in v2:
time: 25.9 us; the launch traced here: 25.8 us
  waiting for transfers between devices  11.8 us (46%)
  starting transfers between devices  11.6 us (45%)
  local copies, waits for them, and re-layouts  1.02 us (4%)
  Pallas kernels  0.75 us (3%)
  other arithmetic  0.52 us (2%)
    ppermute x8, waiting for transfers between devices, shifted(): return lax.ppermute(value, axis, pairs)  11.8 us
    ppermute x8, starting transfers between devices, shifted(): return lax.ppermute(value, axis, pairs)  11.6 us
    unnamed x6, local copies, waits for them, and re-layouts  0.97 us
    pallas_call x1, Pallas kernels, body(): pl.pallas_call(lambda *refs: best_kernel(len(lines), len(one_way), mem_co...  0.7 us
  transfers between devices with their start and end apart: 8, of which 4 were waited for; matrix products, arithmetic and copies ran while one was open for 0% of the time, Pallas kernels for 0%

profile of v2, /device:TPU:0, one launch (start us, length us, event | category | flops | bytes accessed | tf_op | source)
XLA Modules:
  0.0 25.8 jit_solution(11683310124451932733)
XLA Ops:
  0.0 0.0 copy-start
  0.0 0.0 copy-start.1
  0.0 0.0 copy-start.2
  0.0 0.7 %copy-done.1 = s32[128]{0:T(128)S(1)} copy-done((s32[128]{0:T(128)S(1)}, s32[128]{0:T(128)}, u32[]{:S(2)}) %copy-start.1) | copy-done | bytes 536
  0.7 0.0 copy-done.2
  0.7 0.3 copy-done
  1.1 3.1 %collective-permute-start.2 = (bf16[1040,128]{1,0:T(8,128)(2,1)S(1)}, bf16[1040,128]{1,0:T(8,128)(2,1)S(1)}, u32[]{:S(2)}, u32[]{:S(2)}) collective-permute-start(bf16[1040,128]{1,0:T(8,128)(2,1)S(1)} %pack.1.refs_0_.refs_4_), channel_id=1, source_target_pairs={{0,4},{8,12},{4,0},{12,8},{1,5},{9,13},{5,1},{13,9},{2,6},{10,14},... | collective-permute-start | bytes 798728 | tf_op jit(solution)/shard_map/ppermute | solution.py:95
  4.2 1.5 %collective-permute-start.1 = (bf16[1040,128]{1,0:T(8,128)(2,1)S(1)}, bf16[1040,128]{1,0:T(8,128)(2,1)S(1)}, u32[]{:S(2)}, u32[]{:S(2)}) collective-permute-start(bf16[1040,128]{1,0:T(8,128)(2,1)S(1)} %pack.1.refs_0_.refs_4_), channel_id=1, source_target_pairs={{0,2},{2,0},{1,3},{3,1},{4,6},{6,4},{5,7},{7,5},{8,10},{10,8},{9,1... | collective-permute-start | bytes 798728 | tf_op jit(solution)/shard_map/ppermute | solution.py:95
  5.7 2.6 %collective-permute-start.4 = (bf16[1040,128]{1,0:T(8,128)(2,1)S(1)}, bf16[1040,128]{1,0:T(8,128)(2,1)S(1)}, u32[]{:S(2)}, u32[]{:S(2)}) collective-permute-start(bf16[1040,128]{1,0:T(8,128)(2,1)S(1)} %pack.1.refs_0_.refs_4_), channel_id=1, source_target_pairs={{0,8},{8,4},{4,12},{12,0},{1,9},{9,5},{5,13},{13,1},{2,10},{10,6},... | collective-permute-start | bytes 798728 | tf_op jit(solution)/shard_map/ppermute | solution.py:95
  8.2 0.0 collective-permute-start
  8.2 2.7 %collective-permute-done.2.refs_6_ = bf16[1040,128]{1,0:T(8,128)(2,1)S(1)} collective-permute-done((bf16[1040,128]{1,0:T(8,128)(2,1)S(1)}, bf16[1040,128]{1,0:T(8,128)(2,1)S(1)}, u32[]{:S(2)}, u32[]{:S(2)}) %collective-permute-start.2) | collective-permute-done | bytes 266272 | tf_op jit(solution)/shard_map/ppermute | solution.py:95
  11.0 1.1 %collective-permute-done.1.refs_2_ = bf16[1040,128]{1,0:T(8,128)(2,1)S(1)} collective-permute-done((bf16[1040,128]{1,0:T(8,128)(2,1)S(1)}, bf16[1040,128]{1,0:T(8,128)(2,1)S(1)}, u32[]{:S(2)}, u32[]{:S(2)}) %collective-permute-start.1) | collective-permute-done | bytes 266272 | tf_op jit(solution)/shard_map/ppermute | solution.py:95
  12.0 0.0 collective-permute-start.3
  12.0 6.5 %collective-permute-done.4.refs_5_ = bf16[1040,128]{1,0:T(8,128)(2,1)S(1)} collective-permute-done((bf16[1040,128]{1,0:T(8,128)(2,1)S(1)}, bf16[1040,128]{1,0:T(8,128)(2,1)S(1)}, u32[]{:S(2)}, u32[]{:S(2)}) %collective-permute-start.4) | collective-permute-done | bytes 266272 | tf_op jit(solution)/shard_map/ppermute | solution.py:95
  18.6 0.0 collective-permute-done.refs_1_
  18.6 0.0 collective-permute-done.3.refs_3_
  18.6 0.7 %best.1 = (f32[2,128]{1,0:T(2,128)S(1)}, f32[2,128]{1,0:T(2,128)S(1)}, f32[1,128]{1,0:T(1,128)S(1)}) custom-call(bf16[1040,128]{1,0:T(8,128)(2,1)S(1)} %pack.1.refs_0_.refs_4_, bf16[1040,128]{1,0:T(8,128)(2,1)S(1)} %collective-permute-done.refs_1_, bf16[1040,128]{1,0:T(8,128)(2,1)S(1)} %collective-permute-done.1.refs_2_, ...), custom_call_target="tpu_custom_call" | custom-call | tf_op jit(solution)/shard_map/best/pallas_call | solution.py:133
  19.3 1.6 %collective-permute-start.5 = (f32[2,128]{1,0:T(2,128)S(1)}, f32[2,128]{1,0:T(2,128)S(1)}, u32[]{:S(2)}, u32[]{:S(2)}) collective-permute-start(f32[2,128]{1,0:T(2,128)S(1)} %get-tuple-element.17), channel_id=1, source_target_pairs={{0,2},{2,0},{1,3},{3,1},{4,6},{6,4},{5,7},{7,5},{8,10},{10,8},{9,1... | collective-permute-start | bytes 3080 | tf_op jit(solution)/shard_map/ppermute | solution.py:95
  20.8 2.8 %collective-permute-start.7 = (f32[1,128]{1,0:T(1,128)S(1)}, f32[1,128]{1,0:T(1,128)S(1)}, u32[]{:S(2)}, u32[]{:S(2)}) collective-permute-start(f32[1,128]{1,0:T(1,128)S(1)} %get-tuple-element.18), channel_id=1, source_target_pairs={{0,12},{8,0},{4,8},{12,4},{1,13},{9,1},{5,9},{13,5},{2,14},{10,2},... | collective-permute-start | bytes 1544 | tf_op jit(solution)/shard_map/ppermute | solution.py:95
  23.7 0.0 collective-permute-done.5
  23.7 0.1 collective-permute-start.6
  23.8 1.5 %collective-permute-done.7 = f32[1,128]{1,0:T(1,128)S(1)} collective-permute-done((f32[1,128]{1,0:T(1,128)S(1)}, f32[1,128]{1,0:T(1,128)S(1)}, u32[]{:S(2)}, u32[]{:S(2)}) %collective-permute-start.7) | collective-permute-done | bytes 544 | tf_op jit(solution)/shard_map/ppermute | solution.py:95
  25.3 0.0 collective-permute-done.6
  25.3 0.5 %maximum_bitcast_fusion = f32[128]{0:T(128)} fusion(f32[1,128]{1,0:T(1,128)S(1)} %collective-permute-done.7, f32[1,128]{1,0:T(1,128)S(1)} %collective-permute-done.6, f32[2,128]{1,0:T(2,128)S(1)} %max.9), kind=kLoop, calls=%fused_computation.1 | loop fusion | flops 256 | bytes 2048 | tf_op jit(solution)/shard_map/reshape | solution.py:151
  (5 shorter events, 0.1 us)
Async XLA Ops:
  0.0 1.0 %copy-start = (bf16[128,1024]{1,0:T(8,128)(2,1)S(1)}, bf16[128,1024]{1,0:T(8,128)(2,1)}, u32[]{:S(2)}) copy-start(bf16[128,1024]{1,0:T(8,128)(2,1)} %param.3) | copy-start | bytes 786436
  0.0 0.7 %copy-start.1 = (s32[128]{0:T(128)S(1)}, s32[128]{0:T(128)}, u32[]{:S(2)}) copy-start(s32[128]{0:T(128)} %param.4) | copy-start | bytes 1540
  0.0 0.7 %copy-start.2 = (s32[128]{0:T(128)S(1)}, s32[128]{0:T(128)}, u32[]{:S(2)}) copy-start(s32[128]{0:T(128)} %param.5) | copy-start | bytes 1540
  1.1 9.9 %collective-permute-start.2 = (bf16[1040,128]{1,0:T(8,128)(2,1)S(1)}, bf16[1040,128]{1,0:T(8,128)(2,1)S(1)}, u32[]{:S(2)}, u32[]{:S(2)}) collective-permute-start(bf16[1040,128]{1,0:T(8,128)(2,1)S(1)} %pack.1.refs_0_.refs_4_), channel_id=1, source_target_pairs={{0,4},{8,12},{4,0},{12,8},{1,5},{9,13},{5,1},{13,9},{2,6},{10,14},... | collective-permute-start | bytes 798728 | tf_op jit(solution)/shard_map/ppermute | solution.py:95
  4.2 7.9 %collective-permute-start.1 = (bf16[1040,128]{1,0:T(8,128)(2,1)S(1)}, bf16[1040,128]{1,0:T(8,128)(2,1)S(1)}, u32[]{:S(2)}, u32[]{:S(2)}) collective-permute-start(bf16[1040,128]{1,0:T(8,128)(2,1)S(1)} %pack.1.refs_0_.refs_4_), channel_id=1, source_target_pairs={{0,2},{2,0},{1,3},{3,1},{4,6},{6,4},{5,7},{7,5},{8,10},{10,8},{9,1... | collective-permute-start | bytes 798728 | tf_op jit(solution)/shard_map/ppermute | solution.py:95
  5.7 12.9 %collective-permute-start.4 = (bf16[1040,128]{1,0:T(8,128)(2,1)S(1)}, bf16[1040,128]{1,0:T(8,128)(2,1)S(1)}, u32[]{:S(2)}, u32[]{:S(2)}) collective-permute-start(bf16[1040,128]{1,0:T(8,128)(2,1)S(1)} %pack.1.refs_0_.refs_4_), channel_id=1, source_target_pairs={{0,8},{8,4},{4,12},{12,0},{1,9},{9,5},{5,13},{13,1},{2,10},{10,6},... | collective-permute-start | bytes 798728 | tf_op jit(solution)/shard_map/ppermute | solution.py:95
  8.2 10.3 %collective-permute-start = (bf16[1040,128]{1,0:T(8,128)(2,1)S(1)}, bf16[1040,128]{1,0:T(8,128)(2,1)S(1)}, u32[]{:S(2)}, u32[]{:S(2)}) collective-permute-start(bf16[1040,128]{1,0:T(8,128)(2,1)S(1)} %pack.1.refs_0_.refs_4_), channel_id=1, source_target_pairs={{0,1},{1,0},{2,3},{3,2},{4,5},{5,4},{6,7},{7,6},{8,9},{9,8},{10,11... | collective-permute-start | bytes 798728 | tf_op jit(solution)/shard_map/ppermute | solution.py:95
  12.0 6.5 %collective-permute-start.3 = (bf16[1040,128]{1,0:T(8,128)(2,1)S(1)}, bf16[1040,128]{1,0:T(8,128)(2,1)S(1)}, u32[]{:S(2)}, u32[]{:S(2)}) collective-permute-start(bf16[1040,128]{1,0:T(8,128)(2,1)S(1)} %collective-permute-done.1.refs_2_), channel_id=1, source_target_pairs={{0,1},{1,0},{2,3},{3,2},{4,5},{5,4},{6,7},{7,6},{8,9},{9,8},{10,11... | collective-permute-start | bytes 798728 | tf_op jit(solution)/shard_map/ppermute | solution.py:95
  19.3 4.4 %collective-permute-start.5 = (f32[2,128]{1,0:T(2,128)S(1)}, f32[2,128]{1,0:T(2,128)S(1)}, u32[]{:S(2)}, u32[]{:S(2)}) collective-permute-start(f32[2,128]{1,0:T(2,128)S(1)} %get-tuple-element.17), channel_id=1, source_target_pairs={{0,2},{2,0},{1,3},{3,1},{4,6},{6,4},{5,7},{7,5},{8,10},{10,8},{9,1... | collective-permute-start | bytes 3080 | tf_op jit(solution)/shard_map/ppermute | solution.py:95
  20.8 4.4 %collective-permute-start.7 = (f32[1,128]{1,0:T(1,128)S(1)}, f32[1,128]{1,0:T(1,128)S(1)}, u32[]{:S(2)}, u32[]{:S(2)}) collective-permute-start(f32[1,128]{1,0:T(1,128)S(1)} %get-tuple-element.18), channel_id=1, source_target_pairs={{0,12},{8,0},{4,8},{12,4},{1,13},{9,1},{5,9},{13,5},{2,14},{10,2},... | collective-permute-start | bytes 1544 | tf_op jit(solution)/shard_map/ppermute | solution.py:95
  23.7 1.6 %collective-permute-start.6 = (f32[1,128]{1,0:T(1,128)S(1)}, f32[1,128]{1,0:T(1,128)S(1)}, u32[]{:S(2)}, u32[]{:S(2)}) collective-permute-start(f32[1,128]{1,0:T(1,128)S(1)} %slice.7), channel_id=1, source_target_pairs={{0,1},{1,0},{2,3},{3,2},{4,5},{5,4},{6,7},{7,6},{8,9},{9,8},{10,11... | collective-permute-start | bytes 1544 | tf_op jit(solution)/shard_map/ppermute | solution.py:95

commit v3 on v1

--- a/solution.py
+++ b/solution.py
@@ -44,9 +44,16 @@
 
 def best_kernel(line_count, back_count, mem_count, sub_count, *refs):
     plane_count = mem_count * sub_count
-    plane = refs[:plane_count]
-    lines = refs[plane_count : plane_count + line_count]
-    outs = refs[line_count + plane_count :]
+    chip, refs = refs[:sub_count], refs[sub_count:]
+    turned_count = (mem_count - 1) * (sub_count - 1)
+    turned, refs = refs[:turned_count], refs[turned_count:]
+    one_way, refs = refs[:back_count], refs[back_count:]
+    straight, refs = refs[: mem_count - 1], refs[mem_count - 1 :]
+    both_ways, outs = refs[: line_count - 1 - back_count], refs[line_count - 1 - back_count :]
+    lines = chip[:1] + one_way + both_ways
+    plane = list(chip)
+    for index, block in enumerate(straight):
+        plane += [block, *turned[index * (sub_count - 1) : (index + 1) * (sub_count - 1)]]
     plane_outs, back_outs = outs[:mem_count], outs[mem_count:]
     rows = lines[0].shape[1]
 
@@ -122,21 +129,35 @@
     distances = list(range(1, clus_count // 2 + 1))
     one_way = [d for d in distances if 2 * d != clus_count]
     lines = [message] + [shifted(message, "clus", ring, d) for d in distances]
-    plane = []
-    for shift in range(mem_count):
-        block = shifted(message, "mem", mem_order, shift) if shift else message
-        plane.append(block)
-        plane.extend(shifted(block, "sub", sub_order, turn) for turn in range(1, sub_count))
+    def from_plane(value, shift, turn):
+        pairs = [
+            (m * sub_count + c, (m + shift) % mem_count * sub_count + (c + turn) % sub_count)
+            for m in range(mem_count)
+            for c in range(sub_count)
+        ]
+        return lax.ppermute(value, ("mem", "sub"), pairs) if shift or turn else value
+
+    plane = [
+        from_plane(message, shift, turn)
+        for shift in range(mem_count)
+        for turn in range(sub_count)
+    ]
 
     outs = pl.pallas_call(
         lambda *refs: best_kernel(len(lines), len(one_way), mem_count, sub_count, *refs),
         out_shape=[jax.ShapeDtypeStruct((sub_count, row_count), jnp.float32)] * mem_count
         + [jax.ShapeDtypeStruct((1, row_count), jnp.float32)] * len(one_way),
-        in_specs=[vmem] * (len(lines) + len(plane)),
+        in_specs=[vmem] * (len(lines) - 1 + len(plane)),
         out_specs=[vmem] * (mem_count + len(one_way)),
         compiler_params=params,
         name="best",
-    )(*plane, *lines)
+    )(
+        *plane[:sub_count],
+        *[block for index, block in enumerate(plane) if index > sub_count and index % sub_count],
+        *lines[1 : 1 + len(one_way)],
+        *plane[sub_count::sub_count],
+        *lines[1 + len(one_way) :],
+    )
     table = outs[0]
     for shift in range(1, mem_count):
         table = jnp.maximum(table, shifted(outs[shift], "mem", mem_order, -shift))

time: 26.2 us -> 25.9 us (0.989)
  waiting for transfers between devices: 13.4 us -> 11.2 us
  starting transfers between devices: 10.4 us -> 12.3 us
    ppermute x8 -> x5, waiting for transfers between devices: 13.4 us -> 9.41 us  [shifted(): return lax.ppermute(value, axis, pairs)]
    ppermute x0 -> x3, starting transfers between devices: none -> 2.14 us  [from_plane(): lax.ppermute(value, ('mem', 'sub'), pairs)]
    ppermute x0 -> x3, waiting for transfers between devices: none -> 1.77 us  [from_plane(): lax.ppermute(value, ('mem', 'sub'), pairs)]
    ppermute x8 -> x5, starting transfers between devices: 10.4 us -> 10.1 us  [shifted(): return lax.ppermute(value, axis, pairs)]
  transfers between devices with their start and end apart: 8 -> 8, of which waited for: 5 -> 4; matrix products, arithmetic and copies ran while one was open for 0% -> 0% of each run, Pallas kernels for 0% -> 0%
where the time goes in v3:
time: 25.9 us; the launch traced here: 25.8 us
  starting transfers between devices  12.3 us (47%)
  waiting for transfers between devices  11.2 us (43%)
  local copies, waits for them, and re-layouts  1.02 us (4%)
  Pallas kernels  0.74 us (3%)
  other arithmetic  0.52 us (2%)
    ppermute x5, starting transfers between devices, shifted(): return lax.ppermute(value, axis, pairs)  10.1 us
    ppermute x5, waiting for transfers between devices, shifted(): return lax.ppermute(value, axis, pairs)  9.41 us
    ppermute x3, starting transfers between devices, from_plane(): lax.ppermute(value, ('mem', 'sub'), pairs)  2.14 us
    ppermute x3, waiting for transfers between devices, from_plane(): lax.ppermute(value, ('mem', 'sub'), pairs)  1.77 us
    unnamed x6, local copies, waits for them, and re-layouts  0.97 us
    pallas_call x1, Pallas kernels, body(): pl.pallas_call(lambda *refs: best_kernel(len(lines), len(one_way), mem_co...  0.69 us
  transfers between devices with their start and end apart: 8, of which 4 were waited for; matrix products, arithmetic and copies ran while one was open for 0% of the time, Pallas kernels for 0%

profile of v3, /device:TPU:0, one launch (start us, length us, event | category | flops | bytes accessed | tf_op | source)
XLA Modules:
  0.0 25.8 jit_solution(12244104801356716980)
XLA Ops:
  0.0 0.0 copy-start
  0.0 0.0 copy-start.1
  0.0 0.0 copy-start.2
  0.0 0.7 %copy-done.1 = s32[128]{0:T(128)S(1)} copy-done((s32[128]{0:T(128)S(1)}, s32[128]{0:T(128)}, u32[]{:S(2)}) %copy-start.1) | copy-done | bytes 536
  0.7 0.0 copy-done.2
  0.7 0.3 copy-done
  1.1 3.1 %collective-permute-start.4 = (bf16[1040,128]{1,0:T(8,128)(2,1)S(1)}, bf16[1040,128]{1,0:T(8,128)(2,1)S(1)}, u32[]{:S(2)}, u32[]{:S(2)}) collective-permute-start(bf16[1040,128]{1,0:T(8,128)(2,1)S(1)} %pack.1.refs_0_), channel_id=1, source_target_pairs={{0,4},{8,12},{4,0},{12,8},{1,5},{9,13},{5,1},{13,9},{2,6},{10,14},... | collective-permute-start | bytes 798728 | tf_op jit(solution)/shard_map/ppermute | solution.py:102
  4.2 1.5 %collective-permute-start.3 = (bf16[1040,128]{1,0:T(8,128)(2,1)S(1)}, bf16[1040,128]{1,0:T(8,128)(2,1)S(1)}, u32[]{:S(2)}, u32[]{:S(2)}) collective-permute-start(bf16[1040,128]{1,0:T(8,128)(2,1)S(1)} %pack.1.refs_0_), channel_id=1, source_target_pairs={{0,2},{1,3},{2,0},{3,1},{4,6},{5,7},{6,4},{7,5},{8,10},{9,11},{10,... | collective-permute-start | bytes 798728 | tf_op jit(solution)/shard_map/ppermute | solution.py:138
  5.7 2.6 %collective-permute-start.2 = (bf16[1040,128]{1,0:T(8,128)(2,1)S(1)}, bf16[1040,128]{1,0:T(8,128)(2,1)S(1)}, u32[]{:S(2)}, u32[]{:S(2)}) collective-permute-start(bf16[1040,128]{1,0:T(8,128)(2,1)S(1)} %pack.1.refs_0_), channel_id=1, source_target_pairs={{0,8},{8,4},{4,12},{12,0},{1,9},{9,5},{5,13},{13,1},{2,10},{10,6},... | collective-permute-start | bytes 798728 | tf_op jit(solution)/shard_map/ppermute | solution.py:102
  8.2 0.0 collective-permute-start.1
  8.2 0.6 %collective-permute-start = (bf16[1040,128]{1,0:T(8,128)(2,1)S(1)}, bf16[1040,128]{1,0:T(8,128)(2,1)S(1)}, u32[]{:S(2)}, u32[]{:S(2)}) collective-permute-start(bf16[1040,128]{1,0:T(8,128)(2,1)S(1)} %pack.1.refs_0_), channel_id=1, source_target_pairs={{0,1},{1,0},{2,3},{3,2},{4,5},{5,4},{6,7},{7,6},{8,9},{9,8},{10,11... | collective-permute-start | bytes 798728 | tf_op jit(solution)/shard_map/ppermute | solution.py:138
  8.9 2.1 %collective-permute-done.4.refs_5_ = bf16[1040,128]{1,0:T(8,128)(2,1)S(1)} collective-permute-done((bf16[1040,128]{1,0:T(8,128)(2,1)S(1)}, bf16[1040,128]{1,0:T(8,128)(2,1)S(1)}, u32[]{:S(2)}, u32[]{:S(2)}) %collective-permute-start.4) | collective-permute-done | bytes 266272 | tf_op jit(solution)/shard_map/ppermute | solution.py:102
  11.0 1.8 %collective-permute-done.3.refs_4_ = bf16[1040,128]{1,0:T(8,128)(2,1)S(1)} collective-permute-done((bf16[1040,128]{1,0:T(8,128)(2,1)S(1)}, bf16[1040,128]{1,0:T(8,128)(2,1)S(1)}, u32[]{:S(2)}, u32[]{:S(2)}) %collective-permute-start.3) | collective-permute-done | bytes 266272 | tf_op jit(solution)/shard_map/ppermute | solution.py:138
  12.7 5.8 %collective-permute-done.2.refs_3_ = bf16[1040,128]{1,0:T(8,128)(2,1)S(1)} collective-permute-done((bf16[1040,128]{1,0:T(8,128)(2,1)S(1)}, bf16[1040,128]{1,0:T(8,128)(2,1)S(1)}, u32[]{:S(2)}, u32[]{:S(2)}) %collective-permute-start.2) | collective-permute-done | bytes 266272 | tf_op jit(solution)/shard_map/ppermute | solution.py:102
  18.6 0.0 collective-permute-done.1.refs_2_
  18.6 0.0 collective-permute-done.refs_1_
  18.6 0.7 %best.1 = (f32[2,128]{1,0:T(2,128)S(1)}, f32[2,128]{1,0:T(2,128)S(1)}, f32[1,128]{1,0:T(1,128)S(1)}) custom-call(bf16[1040,128]{1,0:T(8,128)(2,1)S(1)} %pack.1.refs_0_, bf16[1040,128]{1,0:T(8,128)(2,1)S(1)} %collective-permute-done.refs_1_, bf16[1040,128]{1,0:T(8,128)(2,1)S(1)} %collective-permute-done.1.refs_2_, ...), custom_call_target="tpu_custom_call" | custom-call | tf_op jit(solution)/shard_map/best/pallas_call | solution.py:146
  19.3 1.6 %collective-permute-start.5 = (f32[2,128]{1,0:T(2,128)S(1)}, f32[2,128]{1,0:T(2,128)S(1)}, u32[]{:S(2)}, u32[]{:S(2)}) collective-permute-start(f32[2,128]{1,0:T(2,128)S(1)} %get-tuple-element.13), channel_id=1, source_target_pairs={{0,2},{2,0},{1,3},{3,1},{4,6},{6,4},{5,7},{7,5},{8,10},{10,8},{9,1... | collective-permute-start | bytes 3080 | tf_op jit(solution)/shard_map/ppermute | solution.py:102
  20.8 2.8 %collective-permute-start.7 = (f32[1,128]{1,0:T(1,128)S(1)}, f32[1,128]{1,0:T(1,128)S(1)}, u32[]{:S(2)}, u32[]{:S(2)}) collective-permute-start(f32[1,128]{1,0:T(1,128)S(1)} %get-tuple-element.14), channel_id=1, source_target_pairs={{0,12},{8,0},{4,8},{12,4},{1,13},{9,1},{5,9},{13,5},{2,14},{10,2},... | collective-permute-start | bytes 1544 | tf_op jit(solution)/shard_map/ppermute | solution.py:102
  23.7 0.0 collective-permute-done.5
  23.7 0.1 collective-permute-start.6
  23.7 1.5 %collective-permute-done.7 = f32[1,128]{1,0:T(1,128)S(1)} collective-permute-done((f32[1,128]{1,0:T(1,128)S(1)}, f32[1,128]{1,0:T(1,128)S(1)}, u32[]{:S(2)}, u32[]{:S(2)}) %collective-permute-start.7) | collective-permute-done | bytes 544 | tf_op jit(solution)/shard_map/ppermute | solution.py:102
  25.3 0.0 collective-permute-done.6
  25.3 0.5 %maximum_bitcast_fusion = f32[128]{0:T(128)} fusion(f32[1,128]{1,0:T(1,128)S(1)} %collective-permute-done.7, f32[1,128]{1,0:T(1,128)S(1)} %collective-permute-done.6, f32[2,128]{1,0:T(2,128)S(1)} %max.9), kind=kLoop, calls=%fused_computation.1 | loop fusion | flops 256 | bytes 2048 | tf_op jit(solution)/shard_map/reshape | solution.py:170
  (5 shorter events, 0.1 us)
Async XLA Ops:
  0.0 1.0 %copy-start = (bf16[128,1024]{1,0:T(8,128)(2,1)S(1)}, bf16[128,1024]{1,0:T(8,128)(2,1)}, u32[]{:S(2)}) copy-start(bf16[128,1024]{1,0:T(8,128)(2,1)} %param.3) | copy-start | bytes 786436
  0.0 0.7 %copy-start.1 = (s32[128]{0:T(128)S(1)}, s32[128]{0:T(128)}, u32[]{:S(2)}) copy-start(s32[128]{0:T(128)} %param.4) | copy-start | bytes 1540
  0.0 0.7 %copy-start.2 = (s32[128]{0:T(128)S(1)}, s32[128]{0:T(128)}, u32[]{:S(2)}) copy-start(s32[128]{0:T(128)} %param.5) | copy-start | bytes 1540
  1.1 9.9 %collective-permute-start.4 = (bf16[1040,128]{1,0:T(8,128)(2,1)S(1)}, bf16[1040,128]{1,0:T(8,128)(2,1)S(1)}, u32[]{:S(2)}, u32[]{:S(2)}) collective-permute-start(bf16[1040,128]{1,0:T(8,128)(2,1)S(1)} %pack.1.refs_0_), channel_id=1, source_target_pairs={{0,4},{8,12},{4,0},{12,8},{1,5},{9,13},{5,1},{13,9},{2,6},{10,14},... | collective-permute-start | bytes 798728 | tf_op jit(solution)/shard_map/ppermute | solution.py:102
  4.2 8.6 %collective-permute-start.3 = (bf16[1040,128]{1,0:T(8,128)(2,1)S(1)}, bf16[1040,128]{1,0:T(8,128)(2,1)S(1)}, u32[]{:S(2)}, u32[]{:S(2)}) collective-permute-start(bf16[1040,128]{1,0:T(8,128)(2,1)S(1)} %pack.1.refs_0_), channel_id=1, source_target_pairs={{0,2},{1,3},{2,0},{3,1},{4,6},{5,7},{6,4},{7,5},{8,10},{9,11},{10,... | collective-permute-start | bytes 798728 | tf_op jit(solution)/shard_map/ppermute | solution.py:138
  5.7 12.9 %collective-permute-start.2 = (bf16[1040,128]{1,0:T(8,128)(2,1)S(1)}, bf16[1040,128]{1,0:T(8,128)(2,1)S(1)}, u32[]{:S(2)}, u32[]{:S(2)}) collective-permute-start(bf16[1040,128]{1,0:T(8,128)(2,1)S(1)} %pack.1.refs_0_), channel_id=1, source_target_pairs={{0,8},{8,4},{4,12},{12,0},{1,9},{9,5},{5,13},{13,1},{2,10},{10,6},... | collective-permute-start | bytes 798728 | tf_op jit(solution)/shard_map/ppermute | solution.py:102
  8.2 10.3 %collective-permute-start.1 = (bf16[1040,128]{1,0:T(8,128)(2,1)S(1)}, bf16[1040,128]{1,0:T(8,128)(2,1)S(1)}, u32[]{:S(2)}, u32[]{:S(2)}) collective-permute-start(bf16[1040,128]{1,0:T(8,128)(2,1)S(1)} %pack.1.refs_0_), channel_id=1, source_target_pairs={{0,3},{1,2},{2,1},{3,0},{4,7},{5,6},{6,5},{7,4},{8,11},{9,10},{10,... | collective-permute-start | bytes 798728 | tf_op jit(solution)/shard_map/ppermute | solution.py:138
  8.2 10.3 %collective-permute-start = (bf16[1040,128]{1,0:T(8,128)(2,1)S(1)}, bf16[1040,128]{1,0:T(8,128)(2,1)S(1)}, u32[]{:S(2)}, u32[]{:S(2)}) collective-permute-start(bf16[1040,128]{1,0:T(8,128)(2,1)S(1)} %pack.1.refs_0_), channel_id=1, source_target_pairs={{0,1},{1,0},{2,3},{3,2},{4,5},{5,4},{6,7},{7,6},{8,9},{9,8},{10,11... | collective-permute-start | bytes 798728 | tf_op jit(solution)/shard_map/ppermute | solution.py:138
  19.3 4.4 %collective-permute-start.5 = (f32[2,128]{1,0:T(2,128)S(1)}, f32[2,128]{1,0:T(2,128)S(1)}, u32[]{:S(2)}, u32[]{:S(2)}) collective-permute-start(f32[2,128]{1,0:T(2,128)S(1)} %get-tuple-element.13), channel_id=1, source_target_pairs={{0,2},{2,0},{1,3},{3,1},{4,6},{6,4},{5,7},{7,5},{8,10},{10,8},{9,1... | collective-permute-start | bytes 3080 | tf_op jit(solution)/shard_map/ppermute | solution.py:102
  20.8 4.4 %collective-permute-start.7 = (f32[1,128]{1,0:T(1,128)S(1)}, f32[1,128]{1,0:T(1,128)S(1)}, u32[]{:S(2)}, u32[]{:S(2)}) collective-permute-start(f32[1,128]{1,0:T(1,128)S(1)} %get-tuple-element.14), channel_id=1, source_target_pairs={{0,12},{8,0},{4,8},{12,4},{1,13},{9,1},{5,9},{13,5},{2,14},{10,2},... | collective-permute-start | bytes 1544 | tf_op jit(solution)/shard_map/ppermute | solution.py:102
  23.7 1.6 %collective-permute-start.6 = (f32[1,128]{1,0:T(1,128)S(1)}, f32[1,128]{1,0:T(1,128)S(1)}, u32[]{:S(2)}, u32[]{:S(2)}) collective-permute-start(f32[1,128]{1,0:T(1,128)S(1)} %slice.7), channel_id=1, source_target_pairs={{0,1},{1,0},{2,3},{3,2},{4,5},{5,4},{6,7},{7,6},{8,9},{9,8},{10,11... | collective-permute-start | bytes 1544 | tf_op jit(solution)/shard_map/ppermute | solution.py:102

commit v4 on v1

--- a/solution.py
+++ b/solution.py
@@ -31,6 +31,12 @@
     copy.wait()
 
 
+def stage_kernel(*refs):
+    half = len(refs) // 2
+    for source, target in zip(refs[:half], refs[half:]):
+        target[...] = source[...]
+
+
 def rows_of(message):
     rows = message.shape[1]
     chunks = message.shape[0] // rows
@@ -44,8 +50,8 @@
 
 def best_kernel(line_count, back_count, mem_count, sub_count, *refs):
     plane_count = mem_count * sub_count
-    plane = refs[:plane_count]
-    lines = refs[plane_count : plane_count + line_count]
+    lines = refs[line_count - 1 : line_count] + refs[: line_count - 1]
+    plane = refs[line_count : line_count + plane_count]
     outs = refs[line_count + plane_count :]
     plane_outs, back_outs = outs[:mem_count], outs[mem_count:]
     rows = lines[0].shape[1]
@@ -122,11 +128,29 @@
     distances = list(range(1, clus_count // 2 + 1))
     one_way = [d for d in distances if 2 * d != clus_count]
     lines = [message] + [shifted(message, "clus", ring, d) for d in distances]
-    plane = []
-    for shift in range(mem_count):
-        block = shifted(message, "mem", mem_order, shift) if shift else message
-        plane.append(block)
-        plane.extend(shifted(block, "sub", sub_order, turn) for turn in range(1, sub_count))
+    def near_blocks(block):
+        near = []
+        for shift in range(mem_count):
+            straight = shifted(block, "mem", mem_order, shift) if shift else block
+            near.extend([straight] if shift else [])
+            near.extend(shifted(straight, "sub", sub_order, t) for t in range(1, sub_count))
+        return near
+
+    near = lax.cond(
+        lax.axis_index("clus") < clus_count,
+        near_blocks,
+        lambda block: [jnp.zeros_like(block)] * (sub_count * mem_count - 1),
+        message,
+    )
+    near = pl.pallas_call(
+        stage_kernel,
+        out_shape=[jax.ShapeDtypeStruct(message.shape, message.dtype)] * len(near),
+        in_specs=[vmem] * len(near),
+        out_specs=[vmem] * len(near),
+        compiler_params=params,
+        name="stage",
+    )(*near)
+    plane = [message, *near]
 
     outs = pl.pallas_call(
         lambda *refs: best_kernel(len(lines), len(one_way), mem_count, sub_count, *refs),
@@ -136,7 +160,7 @@
         out_specs=[vmem] * (mem_count + len(one_way)),
         compiler_params=params,
         name="best",
-    )(*plane, *lines)
+    )(*lines[1:], *lines[:1], *plane)
     table = outs[0]
     for shift in range(1, mem_count):
         table = jnp.maximum(table, shifted(outs[shift], "mem", mem_order, -shift))

time: 26.2 us -> 25.7 us (0.981)
  waiting for transfers between devices: 13.4 us -> 10.9 us
  Pallas kernels: 0.75 us -> 1.9 us
  starting transfers between devices: 10.4 us -> 11.2 us
    ppermute x8, waiting for transfers between devices: 13.4 us -> 10.9 us  [shifted(): return lax.ppermute(value, axis, pairs)]
    pallas_call x0 -> x1, Pallas kernels: none -> 1.16 us  [body(): pl.pallas_call(stage_kernel, out_shape=[jax.ShapeDtypeStruct(message.shap...]
    ppermute x8, starting transfers between devices: 10.4 us -> 11.2 us  [shifted(): return lax.ppermute(value, axis, pairs)]
  transfers between devices with their start and end apart: 8 -> 8, of which waited for: 5 -> 4; matrix products, arithmetic and copies ran while one was open for 0% -> 0% of each run, Pallas kernels for 0% -> 5%
where the time goes in v4:
time: 25.7 us; the launch traced here: 25.6 us
  starting transfers between devices  11.2 us (44%)
  waiting for transfers between devices  10.9 us (42%)
  Pallas kernels  1.9 us (7%)
  local copies, waits for them, and re-layouts  1.02 us (4%)
  other arithmetic  0.52 us (2%)
    ppermute x8, starting transfers between devices, shifted(): return lax.ppermute(value, axis, pairs)  11.2 us
    ppermute x8, waiting for transfers between devices, shifted(): return lax.ppermute(value, axis, pairs)  10.9 us
    pallas_call x1, Pallas kernels, body(): pl.pallas_call(stage_kernel, out_shape=[jax.ShapeDtypeStruct(message.shap...  1.16 us
    unnamed x6, local copies, waits for them, and re-layouts  0.97 us
    pallas_call x1, Pallas kernels, body(): pl.pallas_call(lambda *refs: best_kernel(len(lines), len(one_way), mem_co...  0.69 us
    reshape x1, other arithmetic, body(): return nearest.reshape(row_count)  0.52 us
  transfers between devices with their start and end apart: 8, of which 4 were waited for; matrix products, arithmetic and copies ran while one was open for 0% of the time, Pallas kernels for 5%

profile of v4, /device:TPU:0, one launch (start us, length us, event | category | flops | bytes accessed | tf_op | source)
XLA Modules:
  0.0 25.6 jit_solution(9958650967565906793)
XLA Ops:
  0.0 0.0 copy-start
  0.0 0.0 copy-start.1
  0.0 0.0 copy-start.2
  0.0 0.7 %copy-done.1 = s32[128]{0:T(128)S(1)} copy-done((s32[128]{0:T(128)S(1)}, s32[128]{0:T(128)}, u32[]{:S(2)}) %copy-start.1) | copy-done | bytes 536
  0.7 0.0 copy-done.2
  0.7 0.3 copy-done
  1.1 4.1 %collective-permute-start.3 = (bf16[1040,128]{1,0:T(8,128)(2,1)S(1)}, bf16[1040,128]{1,0:T(8,128)(2,1)S(1)}, u32[]{:S(2)}, u32[]{:S(2)}) collective-permute-start(bf16[1040,128]{1,0:T(8,128)(2,1)S(1)} %pack.1.refs_2_.refs_3_), channel_id=1, source_target_pairs={{0,8},{8,4},{4,12},{12,0},{1,9},{9,5},{5,13},{13,1},{2,10},{10,6},... | collective-permute-start | bytes 798728 | tf_op jit(solution)/shard_map/ppermute | solution.py:101
  5.2 1.6 %collective-permute-start.4 = (bf16[1040,128]{1,0:T(8,128)(2,1)S(1)}, bf16[1040,128]{1,0:T(8,128)(2,1)S(1)}, u32[]{:S(2)}, u32[]{:S(2)}) collective-permute-start(bf16[1040,128]{1,0:T(8,128)(2,1)S(1)} %pack.1.refs_2_.refs_3_), channel_id=1, source_target_pairs={{0,4},{8,12},{4,0},{12,8},{1,5},{9,13},{5,1},{13,9},{2,6},{10,14},... | collective-permute-start | bytes 798728 | tf_op jit(solution)/shard_map/ppermute | solution.py:101
  6.7 9.6 %conditional.1 = (bf16[1040,128]{1,0:T(8,128)(2,1)}, bf16[1040,128]{1,0:T(8,128)(2,1)}, bf16[1040,128]{1,0:T(8,128)(2,1)}) conditional(s32[]{:T(128)} %convert_element_type.3, () %tuple.15, bf16[1040,128]{1,0:T(8,128)(2,1)S(1)} %pack.1.refs_2_.refs_3_), branch_computations={%region_0.0_spmd, %region_1.0_spmd} | conditional | bytes 3195024 | solution.py:139
  6.7 1.5 %collective-permute-start.1 = (bf16[1040,128]{1,0:T(8,128)(2,1)S(1)}, bf16[1040,128]{1,0:T(8,128)(2,1)}, u32[]{:S(2)}, u32[]{:S(2)}) collective-permute-start(bf16[1040,128]{1,0:T(8,128)(2,1)S(1)} %param.1), channel_id=1, source_target_pairs={{0,2},{2,0},{1,3},{3,1},{4,6},{6,4},{5,7},{7,5},{8,10},{10,8},{9,1... | collective-permute-start | bytes 798728 | tf_op jit(solution)/shard_map/cond/branch_1_fun/ppermute | solution.py:101
  8.2 0.0 collective-permute-start
  8.2 6.2 %collective-permute-done.1 = bf16[1040,128]{1,0:T(8,128)(2,1)} collective-permute-done((bf16[1040,128]{1,0:T(8,128)(2,1)S(1)}, bf16[1040,128]{1,0:T(8,128)(2,1)}, u32[]{:S(2)}, u32[]{:S(2)}) %collective-permute-start.1) | collective-permute-done | bytes 266272 | tf_op jit(solution)/shard_map/cond/branch_1_fun/ppermute | solution.py:101
  14.4 0.0 collective-permute-start.2
  14.4 0.0 collective-permute-done
  14.4 1.9 %collective-permute-done.2 = bf16[1040,128]{1,0:T(8,128)(2,1)} collective-permute-done((bf16[1040,128]{1,0:T(8,128)(2,1)}, bf16[1040,128]{1,0:T(8,128)(2,1)}, u32[]{:S(2)}, u32[]{:S(2)}) %collective-permute-start.2) | collective-permute-done | bytes 266272 | tf_op jit(solution)/shard_map/cond/branch_1_fun/ppermute | solution.py:101
  16.3 1.2 %stage.1 = (bf16[1040,128]{1,0:T(8,128)(2,1)S(1)}, bf16[1040,128]{1,0:T(8,128)(2,1)S(1)}, bf16[1040,128]{1,0:T(8,128)(2,1)S(1)}) custom-call(bf16[1040,128]{1,0:T(8,128)(2,1)} %get-tuple-element.19.refs_0_, bf16[1040,128]{1,0:T(8,128)(2,1)} %get-tuple-element.20.refs_1_, bf16[1040,128]{1,0:T(8,128)(2,1)} %get-tuple-element.21.refs_2_), custom_call_target="tpu_custom_call" | custom-call | tf_op jit(solution)/shard_map/stage/pallas_call | solution.py:145
  17.5 0.0 collective-permute-done.3.refs_0_
  17.5 0.9 %collective-permute-done.4.refs_1_ = bf16[1040,128]{1,0:T(8,128)(2,1)S(1)} collective-permute-done((bf16[1040,128]{1,0:T(8,128)(2,1)S(1)}, bf16[1040,128]{1,0:T(8,128)(2,1)S(1)}, u32[]{:S(2)}, u32[]{:S(2)}) %collective-permute-start.4) | collective-permute-done | bytes 266272 | tf_op jit(solution)/shard_map/ppermute | solution.py:101
  18.4 0.7 %best.1 = (f32[2,128]{1,0:T(2,128)S(1)}, f32[2,128]{1,0:T(2,128)S(1)}, f32[1,128]{1,0:T(1,128)S(1)}) custom-call(bf16[1040,128]{1,0:T(8,128)(2,1)S(1)} %collective-permute-done.3.refs_0_, bf16[1040,128]{1,0:T(8,128)(2,1)S(1)} %collective-permute-done.4.refs_1_, bf16[1040,128]{1,0:T(8,128)(2,1)S(1)} %pack.1.refs_2_.refs_3_, ...), custom_call_target="tpu_custom_call" | custom-call | tf_op jit(solution)/shard_map/best/pallas_call | solution.py:155
  19.1 1.6 %collective-permute-start.5 = (f32[2,128]{1,0:T(2,128)S(1)}, f32[2,128]{1,0:T(2,128)S(1)}, u32[]{:S(2)}, u32[]{:S(2)}) collective-permute-start(f32[2,128]{1,0:T(2,128)S(1)} %get-tuple-element.26), channel_id=1, source_target_pairs={{0,2},{2,0},{1,3},{3,1},{4,6},{6,4},{5,7},{7,5},{8,10},{10,8},{9,1... | collective-permute-start | bytes 3080 | tf_op jit(solution)/shard_map/ppermute | solution.py:101
  20.6 2.4 %collective-permute-start.7 = (f32[1,128]{1,0:T(1,128)S(1)}, f32[1,128]{1,0:T(1,128)S(1)}, u32[]{:S(2)}, u32[]{:S(2)}) collective-permute-start(f32[1,128]{1,0:T(1,128)S(1)} %get-tuple-element.27), channel_id=1, source_target_pairs={{0,12},{8,0},{4,8},{12,4},{1,13},{9,1},{5,9},{13,5},{2,14},{10,2},... | collective-permute-start | bytes 1544 | tf_op jit(solution)/shard_map/ppermute | solution.py:101
  23.1 0.0 collective-permute-done.5
  23.1 0.1 collective-permute-start.6
  23.1 1.9 %collective-permute-done.7 = f32[1,128]{1,0:T(1,128)S(1)} collective-permute-done((f32[1,128]{1,0:T(1,128)S(1)}, f32[1,128]{1,0:T(1,128)S(1)}, u32[]{:S(2)}, u32[]{:S(2)}) %collective-permute-start.7) | collective-permute-done | bytes 544 | tf_op jit(solution)/shard_map/ppermute | solution.py:101
  25.1 0.0 collective-permute-done.6
  25.1 0.5 %maximum_bitcast_fusion = f32[128]{0:T(128)} fusion(f32[1,128]{1,0:T(1,128)S(1)} %collective-permute-done.7, f32[1,128]{1,0:T(1,128)S(1)} %collective-permute-done.6, f32[2,128]{1,0:T(2,128)S(1)} %max.9), kind=kLoop, calls=%fused_computation.1 | loop fusion | flops 256 | bytes 2048 | tf_op jit(solution)/shard_map/reshape | solution.py:173
  (5 shorter events, 0.1 us)
Async XLA Ops:
  0.0 1.0 %copy-start = (bf16[128,1024]{1,0:T(8,128)(2,1)S(1)}, bf16[128,1024]{1,0:T(8,128)(2,1)}, u32[]{:S(2)}) copy-start(bf16[128,1024]{1,0:T(8,128)(2,1)} %param.5) | copy-start | bytes 786436
  0.0 0.7 %copy-start.1 = (s32[128]{0:T(128)S(1)}, s32[128]{0:T(128)}, u32[]{:S(2)}) copy-start(s32[128]{0:T(128)} %param.6) | copy-start | bytes 1540
  0.0 0.7 %copy-start.2 = (s32[128]{0:T(128)S(1)}, s32[128]{0:T(128)}, u32[]{:S(2)}) copy-start(s32[128]{0:T(128)} %param.7) | copy-start | bytes 1540
  1.1 16.4 %collective-permute-start.3 = (bf16[1040,128]{1,0:T(8,128)(2,1)S(1)}, bf16[1040,128]{1,0:T(8,128)(2,1)S(1)}, u32[]{:S(2)}, u32[]{:S(2)}) collective-permute-start(bf16[1040,128]{1,0:T(8,128)(2,1)S(1)} %pack.1.refs_2_.refs_3_), channel_id=1, source_target_pairs={{0,8},{8,4},{4,12},{12,0},{1,9},{9,5},{5,13},{13,1},{2,10},{10,6},... | collective-permute-start | bytes 798728 | tf_op jit(solution)/shard_map/ppermute | solution.py:101
  5.2 13.2 %collective-permute-start.4 = (bf16[1040,128]{1,0:T(8,128)(2,1)S(1)}, bf16[1040,128]{1,0:T(8,128)(2,1)S(1)}, u32[]{:S(2)}, u32[]{:S(2)}) collective-permute-start(bf16[1040,128]{1,0:T(8,128)(2,1)S(1)} %pack.1.refs_2_.refs_3_), channel_id=1, source_target_pairs={{0,4},{8,12},{4,0},{12,8},{1,5},{9,13},{5,1},{13,9},{2,6},{10,14},... | collective-permute-start | bytes 798728 | tf_op jit(solution)/shard_map/ppermute | solution.py:101
  6.7 7.7 %collective-permute-start.1 = (bf16[1040,128]{1,0:T(8,128)(2,1)S(1)}, bf16[1040,128]{1,0:T(8,128)(2,1)}, u32[]{:S(2)}, u32[]{:S(2)}) collective-permute-start(bf16[1040,128]{1,0:T(8,128)(2,1)S(1)} %param.1), channel_id=1, source_target_pairs={{0,2},{2,0},{1,3},{3,1},{4,6},{6,4},{5,7},{7,5},{8,10},{10,8},{9,1... | collective-permute-start | bytes 798728 | tf_op jit(solution)/shard_map/cond/branch_1_fun/ppermute | solution.py:101
  8.2 6.2 %collective-permute-start = (bf16[1040,128]{1,0:T(8,128)(2,1)S(1)}, bf16[1040,128]{1,0:T(8,128)(2,1)}, u32[]{:S(2)}, u32[]{:S(2)}) collective-permute-start(bf16[1040,128]{1,0:T(8,128)(2,1)S(1)} %param.1), channel_id=1, source_target_pairs={{0,1},{1,0},{2,3},{3,2},{4,5},{5,4},{6,7},{7,6},{8,9},{9,8},{10,11... | collective-permute-start | bytes 798728 | tf_op jit(solution)/shard_map/cond/branch_1_fun/ppermute | solution.py:101
  14.4 1.9 %collective-permute-start.2 = (bf16[1040,128]{1,0:T(8,128)(2,1)}, bf16[1040,128]{1,0:T(8,128)(2,1)}, u32[]{:S(2)}, u32[]{:S(2)}) collective-permute-start(bf16[1040,128]{1,0:T(8,128)(2,1)} %collective-permute-done.1), channel_id=1, source_target_pairs={{0,1},{1,0},{2,3},{3,2},{4,5},{5,4},{6,7},{7,6},{8,9},{9,8},{10,11... | collective-permute-start | bytes 798728 | tf_op jit(solution)/shard_map/cond/branch_1_fun/ppermute | solution.py:101
  19.1 4.0 %collective-permute-start.5 = (f32[2,128]{1,0:T(2,128)S(1)}, f32[2,128]{1,0:T(2,128)S(1)}, u32[]{:S(2)}, u32[]{:S(2)}) collective-permute-start(f32[2,128]{1,0:T(2,128)S(1)} %get-tuple-element.26), channel_id=1, source_target_pairs={{0,2},{2,0},{1,3},{3,1},{4,6},{6,4},{5,7},{7,5},{8,10},{10,8},{9,1... | collective-permute-start | bytes 3080 | tf_op jit(solution)/shard_map/ppermute | solution.py:101
  20.6 4.4 %collective-permute-start.7 = (f32[1,128]{1,0:T(1,128)S(1)}, f32[1,128]{1,0:T(1,128)S(1)}, u32[]{:S(2)}, u32[]{:S(2)}) collective-permute-start(f32[1,128]{1,0:T(1,128)S(1)} %get-tuple-element.27), channel_id=1, source_target_pairs={{0,12},{8,0},{4,8},{12,4},{1,13},{9,1},{5,9},{13,5},{2,14},{10,2},... | collective-permute-start | bytes 1544 | tf_op jit(solution)/shard_map/ppermute | solution.py:101
  23.1 2.0 %collective-permute-start.6 = (f32[1,128]{1,0:T(1,128)S(1)}, f32[1,128]{1,0:T(1,128)S(1)}, u32[]{:S(2)}, u32[]{:S(2)}) collective-permute-start(f32[1,128]{1,0:T(1,128)S(1)} %slice.7), channel_id=1, source_target_pairs={{0,1},{1,0},{2,3},{3,2},{4,5},{5,4},{6,7},{7,6},{8,9},{9,8},{10,11... | collective-permute-start | bytes 1544 | tf_op jit(solution)/shard_map/ppermute | solution.py:101

commit v5 on v4

--- a/solution.py
+++ b/solution.py
@@ -48,11 +48,11 @@
     return meta[0:1], meta[1:2] * DIGIT + meta[2:3]
 
 
-def best_kernel(line_count, back_count, mem_count, sub_count, *refs):
+def best_kernel(line_count, back_count, table_count, mem_count, sub_count, *refs):
     plane_count = mem_count * sub_count
-    lines = refs[line_count - 1 : line_count] + refs[: line_count - 1]
-    plane = refs[line_count : line_count + plane_count]
-    outs = refs[line_count + plane_count :]
+    lines, refs = refs[:line_count], refs[line_count:]
+    plane, refs = refs[:plane_count], refs[plane_count:]
+    tables, outs = refs[:table_count], refs[table_count:]
     plane_outs, back_outs = outs[:mem_count], outs[mem_count:]
     rows = lines[0].shape[1]
 
@@ -76,9 +76,12 @@
     best = jnp.max(forward, axis=0, keepdims=True)
     for block in range(plane_count):
         shift, turn = block // sub_count, block % sub_count
-        plane_outs[shift][turn : turn + 1, :] = best[:, block * rows : (block + 1) * rows]
+        part = best[:, block * rows : (block + 1) * rows]
+        if table_count:
+            part = jnp.maximum(part, tables[shift][turn : turn + 1, :])
+        plane_outs[shift][turn : turn + 1, :] = part
     for index in range(back_count):
-        piece = slice((index + 1) * rows, (index + 2) * rows)
+        piece = slice(index * rows, (index + 1) * rows)
         backward = jnp.where(line_rank[piece] > rank, scores[piece], NONE)
         back = backward[:, :rows]
         for block in range(1, plane_count):
@@ -152,23 +155,35 @@
     )(*near)
     plane = [message, *near]
 
-    outs = pl.pallas_call(
-        lambda *refs: best_kernel(len(lines), len(one_way), mem_count, sub_count, *refs),
-        out_shape=[jax.ShapeDtypeStruct((sub_count, row_count), jnp.float32)] * mem_count
-        + [jax.ShapeDtypeStruct((1, row_count), jnp.float32)] * len(one_way),
-        in_specs=[vmem] * (len(lines) + len(plane)),
-        out_specs=[vmem] * (mem_count + len(one_way)),
-        compiler_params=params,
-        name="best",
-    )(*lines[1:], *lines[:1], *plane)
-    table = outs[0]
+    def best_of(lines, back_count, tables):
+        operands = [*lines, *plane, *tables]
+        outs = pl.pallas_call(
+            lambda *refs: best_kernel(
+                len(lines), back_count, len(tables), mem_count, sub_count, *refs
+            ),
+            out_shape=[jax.ShapeDtypeStruct((sub_count, row_count), jnp.float32)] * mem_count
+            + [jax.ShapeDtypeStruct((1, row_count), jnp.float32)] * back_count,
+            in_specs=[vmem] * len(operands),
+            out_specs=[vmem] * (mem_count + back_count),
+            compiler_params=params,
+            name="best",
+        )(*operands)
+        return outs[:mem_count], outs[mem_count:]
+
+    tables, _ = best_of(lines[:1], 0, [])
+    backs = []
+    if one_way:
+        tables, backs = best_of(lines[1 : 1 + len(one_way)], len(one_way), tables)
+    if len(lines) > 1 + len(one_way):
+        tables, _ = best_of(lines[1 + len(one_way) :], 0, tables)
+    table = tables[0]
     for shift in range(1, mem_count):
-        table = jnp.maximum(table, shifted(outs[shift], "mem", mem_order, -shift))
+        table = jnp.maximum(table, shifted(tables[shift], "mem", mem_order, -shift))
     nearest = table[0:1]
     for turn in range(1, sub_count):
         part = shifted(table[turn : turn + 1], "sub", sub_order, -turn)
         nearest = jnp.maximum(nearest, part)
-    for distance, value in zip(one_way, outs[mem_count:]):
+    for distance, value in zip(one_way, backs):
         nearest = jnp.maximum(nearest, shifted(value, "clus", ring, -distance))
     return nearest.reshape(row_count)
 

time: 25.7 us -> 25.8 us (level)
  waiting for transfers between devices: 10.9 us -> 9.62 us
  Pallas kernels: 1.9 us -> 2.78 us
  starting transfers between devices: 11.2 us -> 11.6 us
    ppermute x8, waiting for transfers between devices: 10.9 us -> 9.62 us  [shifted(): return lax.ppermute(value, axis, pairs)]
    pallas_call x1 -> x3, Pallas kernels: 0.69 us -> 1.57 us  [best_of(): pl.pallas_call(lambda *refs: best_kernel(len(lines), back_count, len(tabl...]
    ppermute x8, starting transfers between devices: 11.2 us -> 11.6 us  [shifted(): return lax.ppermute(value, axis, pairs)]
  transfers between devices with their start and end apart: 8 -> 8, of which waited for: 4 -> 3; matrix products, arithmetic and copies ran while one was open for 0% -> 0% of each run, Pallas kernels for 5% -> 9%
where the time goes in v5:
time: 25.8 us; the launch traced here: 25.6 us
  starting transfers between devices  11.6 us (45%)
  waiting for transfers between devices  9.62 us (37%)
  Pallas kernels  2.78 us (11%)
  local copies, waits for them, and re-layouts  1.02 us (4%)
  other arithmetic  0.52 us (2%)
    ppermute x8, starting transfers between devices, shifted(): return lax.ppermute(value, axis, pairs)  11.6 us
    ppermute x8, waiting for transfers between devices, shifted(): return lax.ppermute(value, axis, pairs)  9.62 us
    pallas_call x3, Pallas kernels, best_of(): pl.pallas_call(lambda *refs: best_kernel(len(lines), back_count, len(tabl...  1.57 us
    pallas_call x1, Pallas kernels, body(): pl.pallas_call(stage_kernel, out_shape=[jax.ShapeDtypeStruct(message.shap...  1.16 us
    unnamed x6, local copies, waits for them, and re-layouts  0.97 us
  transfers between devices with their start and end apart: 8, of which 3 were waited for; matrix products, arithmetic and copies ran while one was open for 0% of the time, Pallas kernels for 9%

profile of v5, /device:TPU:0, one launch (start us, length us, event | category | flops | bytes accessed | tf_op | source)
XLA Modules:
  0.0 25.6 jit_solution(15681015690154903672)
XLA Ops:
  0.0 0.0 copy-start
  0.0 0.0 copy-start.1
  0.0 0.0 copy-start.2
  0.0 0.7 %copy-done.1 = s32[128]{0:T(128)S(1)} copy-done((s32[128]{0:T(128)S(1)}, s32[128]{0:T(128)}, u32[]{:S(2)}) %copy-start.1) | copy-done | bytes 536
  0.7 0.0 copy-done.2
  0.7 0.3 copy-done
  1.1 4.1 %collective-permute-start.4 = (bf16[1040,128]{1,0:T(8,128)(2,1)S(1)}, bf16[1040,128]{1,0:T(8,128)(2,1)S(1)}, u32[]{:S(2)}, u32[]{:S(2)}) collective-permute-start(bf16[1040,128]{1,0:T(8,128)(2,1)S(1)} %pack.1.refs_0_.refs_1_), channel_id=1, source_target_pairs={{0,8},{8,4},{4,12},{12,0},{1,9},{9,5},{5,13},{13,1},{2,10},{10,6},... | collective-permute-start | bytes 798728 | tf_op jit(solution)/shard_map/ppermute | solution.py:104
  5.2 1.6 %collective-permute-start.3 = (bf16[1040,128]{1,0:T(8,128)(2,1)S(1)}, bf16[1040,128]{1,0:T(8,128)(2,1)S(1)}, u32[]{:S(2)}, u32[]{:S(2)}) collective-permute-start(bf16[1040,128]{1,0:T(8,128)(2,1)S(1)} %pack.1.refs_0_.refs_1_), channel_id=1, source_target_pairs={{0,4},{8,12},{4,0},{12,8},{1,5},{9,13},{5,1},{13,9},{2,6},{10,14},... | collective-permute-start | bytes 798728 | tf_op jit(solution)/shard_map/ppermute | solution.py:104
  6.7 9.6 %conditional.1 = (bf16[1040,128]{1,0:T(8,128)(2,1)}, bf16[1040,128]{1,0:T(8,128)(2,1)}, bf16[1040,128]{1,0:T(8,128)(2,1)}) conditional(s32[]{:T(128)} %convert_element_type.3, () %tuple.15, bf16[1040,128]{1,0:T(8,128)(2,1)S(1)} %pack.1.refs_0_.refs_1_), branch_computations={%region_0.0_spmd, %region_1.0_spmd} | conditional | bytes 3195024 | solution.py:142
  6.7 1.5 %collective-permute-start.1 = (bf16[1040,128]{1,0:T(8,128)(2,1)S(1)}, bf16[1040,128]{1,0:T(8,128)(2,1)}, u32[]{:S(2)}, u32[]{:S(2)}) collective-permute-start(bf16[1040,128]{1,0:T(8,128)(2,1)S(1)} %param.1), channel_id=1, source_target_pairs={{0,2},{2,0},{1,3},{3,1},{4,6},{6,4},{5,7},{7,5},{8,10},{10,8},{9,1... | collective-permute-start | bytes 798728 | tf_op jit(solution)/shard_map/cond/branch_1_fun/ppermute | solution.py:104
  8.2 0.0 collective-permute-start
  8.2 6.2 %collective-permute-done.1 = bf16[1040,128]{1,0:T(8,128)(2,1)} collective-permute-done((bf16[1040,128]{1,0:T(8,128)(2,1)S(1)}, bf16[1040,128]{1,0:T(8,128)(2,1)}, u32[]{:S(2)}, u32[]{:S(2)}) %collective-permute-start.1) | collective-permute-done | bytes 266272 | tf_op jit(solution)/shard_map/cond/branch_1_fun/ppermute | solution.py:104
  14.4 0.0 collective-permute-start.2
  14.4 0.0 collective-permute-done
  14.4 1.9 %collective-permute-done.2 = bf16[1040,128]{1,0:T(8,128)(2,1)} collective-permute-done((bf16[1040,128]{1,0:T(8,128)(2,1)}, bf16[1040,128]{1,0:T(8,128)(2,1)}, u32[]{:S(2)}, u32[]{:S(2)}) %collective-permute-start.2) | collective-permute-done | bytes 266272 | tf_op jit(solution)/shard_map/cond/branch_1_fun/ppermute | solution.py:104
  16.3 1.2 %stage.1 = (bf16[1040,128]{1,0:T(8,128)(2,1)S(1)}, bf16[1040,128]{1,0:T(8,128)(2,1)S(1)}, bf16[1040,128]{1,0:T(8,128)(2,1)S(1)}) custom-call(bf16[1040,128]{1,0:T(8,128)(2,1)} %get-tuple-element.23.refs_0_, bf16[1040,128]{1,0:T(8,128)(2,1)} %get-tuple-element.24.refs_1_, bf16[1040,128]{1,0:T(8,128)(2,1)} %get-tuple-element.25.refs_2_), custom_call_target="tpu_custom_call" | custom-call | tf_op jit(solution)/shard_map/stage/pallas_call | solution.py:148
  17.5 0.5 %best.3 = (f32[2,128]{1,0:T(2,128)S(1)}, f32[2,128]{1,0:T(2,128)S(1)}) custom-call(bf16[1040,128]{1,0:T(8,128)(2,1)S(1)} %pack.1.refs_0_.refs_1_, bf16[1040,128]{1,0:T(8,128)(2,1)S(1)} %pack.1.refs_0_.refs_1_, bf16[1040,128]{1,0:T(8,128)(2,1)S(1)} %get-tuple-element.26.refs_2_, bf16[1040,128]{1,0:T(8,128)(2,1)S(1)} %get-tuple-element.27.refs_3_, ...), custom_call_target="tpu_custom_call" | custom-call | tf_op jit(solution)/shard_map/best/pallas_call | solution.py:160
  18.0 0.0 collective-permute-done.4.refs_0_
  18.0 0.6 %best.4 = (f32[2,128]{1,0:T(2,128)S(1)}, f32[2,128]{1,0:T(2,128)S(1)}, f32[1,128]{1,0:T(1,128)S(1)}) custom-call(bf16[1040,128]{1,0:T(8,128)(2,1)S(1)} %collective-permute-done.4.refs_0_, bf16[1040,128]{1,0:T(8,128)(2,1)S(1)} %pack.1.refs_0_.refs_1_, bf16[1040,128]{1,0:T(8,128)(2,1)S(1)} %get-tuple-element.26.refs_2_, ...), custom_call_target="tpu_custom_call" | custom-call | tf_op jit(solution)/shard_map/best/pallas_call | solution.py:160
  18.6 0.0 collective-permute-done.3.refs_0_
  18.6 0.5 %best.5 = (f32[2,128]{1,0:T(2,128)S(1)}, f32[2,128]{1,0:T(2,128)S(1)}) custom-call(bf16[1040,128]{1,0:T(8,128)(2,1)S(1)} %collective-permute-done.3.refs_0_, bf16[1040,128]{1,0:T(8,128)(2,1)S(1)} %pack.1.refs_0_.refs_1_, bf16[1040,128]{1,0:T(8,128)(2,1)S(1)} %get-tuple-element.26.refs_2_, bf16[1040,128]{1,0:T(8,128)(2,1)S(1)} %get-tuple-element.27.refs_3_, ...), custom_call_target="tpu_custom_call" | custom-call | tf_op jit(solution)/shard_map/best/pallas_call | solution.py:160
  19.1 1.6 %collective-permute-start.5 = (f32[2,128]{1,0:T(2,128)S(1)}, f32[2,128]{1,0:T(2,128)S(1)}, u32[]{:S(2)}, u32[]{:S(2)}) collective-permute-start(f32[2,128]{1,0:T(2,128)S(1)} %get-tuple-element.34), channel_id=1, source_target_pairs={{0,2},{2,0},{1,3},{3,1},{4,6},{6,4},{5,7},{7,5},{8,10},{10,8},{9,1... | collective-permute-start | bytes 3080 | tf_op jit(solution)/shard_map/ppermute | solution.py:104
  20.6 2.8 %collective-permute-start.7 = (f32[1,128]{1,0:T(1,128)S(1)}, f32[1,128]{1,0:T(1,128)S(1)}, u32[]{:S(2)}, u32[]{:S(2)}) collective-permute-start(f32[1,128]{1,0:T(1,128)S(1)} %get-tuple-element.35), channel_id=1, source_target_pairs={{0,12},{8,0},{4,8},{12,4},{1,13},{9,1},{5,9},{13,5},{2,14},{10,2},... | collective-permute-start | bytes 1544 | tf_op jit(solution)/shard_map/ppermute | solution.py:104
  23.5 0.0 collective-permute-done.5
  23.5 0.1 collective-permute-start.6
  23.5 1.5 %collective-permute-done.7 = f32[1,128]{1,0:T(1,128)S(1)} collective-permute-done((f32[1,128]{1,0:T(1,128)S(1)}, f32[1,128]{1,0:T(1,128)S(1)}, u32[]{:S(2)}, u32[]{:S(2)}) %collective-permute-start.7) | collective-permute-done | bytes 544 | tf_op jit(solution)/shard_map/ppermute | solution.py:104
  25.1 0.0 collective-permute-done.6
  25.1 0.5 %maximum_bitcast_fusion = f32[128]{0:T(128)} fusion(f32[1,128]{1,0:T(1,128)S(1)} %collective-permute-done.7, f32[1,128]{1,0:T(1,128)S(1)} %collective-permute-done.6, f32[2,128]{1,0:T(2,128)S(1)} %max.9), kind=kLoop, calls=%fused_computation.1 | loop fusion | flops 256 | bytes 2048 | tf_op jit(solution)/shard_map/reshape | solution.py:188
  (5 shorter events, 0.1 us)
Async XLA Ops:
  0.0 1.0 %copy-start = (bf16[128,1024]{1,0:T(8,128)(2,1)S(1)}, bf16[128,1024]{1,0:T(8,128)(2,1)}, u32[]{:S(2)}) copy-start(bf16[128,1024]{1,0:T(8,128)(2,1)} %param.5) | copy-start | bytes 786436
  0.0 0.7 %copy-start.1 = (s32[128]{0:T(128)S(1)}, s32[128]{0:T(128)}, u32[]{:S(2)}) copy-start(s32[128]{0:T(128)} %param.6) | copy-start | bytes 1540
  0.0 0.7 %copy-start.2 = (s32[128]{0:T(128)S(1)}, s32[128]{0:T(128)}, u32[]{:S(2)}) copy-start(s32[128]{0:T(128)} %param.7) | copy-start | bytes 1540
  1.1 16.9 %collective-permute-start.4 = (bf16[1040,128]{1,0:T(8,128)(2,1)S(1)}, bf16[1040,128]{1,0:T(8,128)(2,1)S(1)}, u32[]{:S(2)}, u32[]{:S(2)}) collective-permute-start(bf16[1040,128]{1,0:T(8,128)(2,1)S(1)} %pack.1.refs_0_.refs_1_), channel_id=1, source_target_pairs={{0,8},{8,4},{4,12},{12,0},{1,9},{9,5},{5,13},{13,1},{2,10},{10,6},... | collective-permute-start | bytes 798728 | tf_op jit(solution)/shard_map/ppermute | solution.py:104
  5.2 13.4 %collective-permute-start.3 = (bf16[1040,128]{1,0:T(8,128)(2,1)S(1)}, bf16[1040,128]{1,0:T(8,128)(2,1)S(1)}, u32[]{:S(2)}, u32[]{:S(2)}) collective-permute-start(bf16[1040,128]{1,0:T(8,128)(2,1)S(1)} %pack.1.refs_0_.refs_1_), channel_id=1, source_target_pairs={{0,4},{8,12},{4,0},{12,8},{1,5},{9,13},{5,1},{13,9},{2,6},{10,14},... | collective-permute-start | bytes 798728 | tf_op jit(solution)/shard_map/ppermute | solution.py:104
  6.7 7.7 %collective-permute-start.1 = (bf16[1040,128]{1,0:T(8,128)(2,1)S(1)}, bf16[1040,128]{1,0:T(8,128)(2,1)}, u32[]{:S(2)}, u32[]{:S(2)}) collective-permute-start(bf16[1040,128]{1,0:T(8,128)(2,1)S(1)} %param.1), channel_id=1, source_target_pairs={{0,2},{2,0},{1,3},{3,1},{4,6},{6,4},{5,7},{7,5},{8,10},{10,8},{9,1... | collective-permute-start | bytes 798728 | tf_op jit(solution)/shard_map/cond/branch_1_fun/ppermute | solution.py:104
  8.2 6.2 %collective-permute-start = (bf16[1040,128]{1,0:T(8,128)(2,1)S(1)}, bf16[1040,128]{1,0:T(8,128)(2,1)}, u32[]{:S(2)}, u32[]{:S(2)}) collective-permute-start(bf16[1040,128]{1,0:T(8,128)(2,1)S(1)} %param.1), channel_id=1, source_target_pairs={{0,1},{1,0},{2,3},{3,2},{4,5},{5,4},{6,7},{7,6},{8,9},{9,8},{10,11... | collective-permute-start | bytes 798728 | tf_op jit(solution)/shard_map/cond/branch_1_fun/ppermute | solution.py:104
  14.4 1.9 %collective-permute-start.2 = (bf16[1040,128]{1,0:T(8,128)(2,1)}, bf16[1040,128]{1,0:T(8,128)(2,1)}, u32[]{:S(2)}, u32[]{:S(2)}) collective-permute-start(bf16[1040,128]{1,0:T(8,128)(2,1)} %collective-permute-done.1), channel_id=1, source_target_pairs={{0,1},{1,0},{2,3},{3,2},{4,5},{5,4},{6,7},{7,6},{8,9},{9,8},{10,11... | collective-permute-start | bytes 798728 | tf_op jit(solution)/shard_map/cond/branch_1_fun/ppermute | solution.py:104
  19.1 4.4 %collective-permute-start.5 = (f32[2,128]{1,0:T(2,128)S(1)}, f32[2,128]{1,0:T(2,128)S(1)}, u32[]{:S(2)}, u32[]{:S(2)}) collective-permute-start(f32[2,128]{1,0:T(2,128)S(1)} %get-tuple-element.34), channel_id=1, source_target_pairs={{0,2},{2,0},{1,3},{3,1},{4,6},{6,4},{5,7},{7,5},{8,10},{10,8},{9,1... | collective-permute-start | bytes 3080 | tf_op jit(solution)/shard_map/ppermute | solution.py:104
  20.6 4.4 %collective-permute-start.7 = (f32[1,128]{1,0:T(1,128)S(1)}, f32[1,128]{1,0:T(1,128)S(1)}, u32[]{:S(2)}, u32[]{:S(2)}) collective-permute-start(f32[1,128]{1,0:T(1,128)S(1)} %get-tuple-element.35), channel_id=1, source_target_pairs={{0,12},{8,0},{4,8},{12,4},{1,13},{9,1},{5,9},{13,5},{2,14},{10,2},... | collective-permute-start | bytes 1544 | tf_op jit(solution)/shard_map/ppermute | solution.py:104
  23.5 1.6 %collective-permute-start.6 = (f32[1,128]{1,0:T(1,128)S(1)}, f32[1,128]{1,0:T(1,128)S(1)}, u32[]{:S(2)}, u32[]{:S(2)}) collective-permute-start(f32[1,128]{1,0:T(1,128)S(1)} %slice.7), channel_id=1, source_target_pairs={{0,1},{1,0},{2,3},{3,2},{4,5},{5,4},{6,7},{7,6},{8,9},{9,8},{10,11... | collective-permute-start | bytes 1544 | tf_op jit(solution)/shard_map/ppermute | solution.py:104

commit v6 on v5

--- a/solution.py
+++ b/solution.py
@@ -170,10 +170,8 @@
         )(*operands)
         return outs[:mem_count], outs[mem_count:]
 
-    tables, _ = best_of(lines[:1], 0, [])
-    backs = []
-    if one_way:
-        tables, backs = best_of(lines[1 : 1 + len(one_way)], len(one_way), tables)
+    near_lines = lines[1 : 1 + len(one_way)] + lines[:1]
+    tables, backs = best_of(near_lines, len(one_way), [])
     if len(lines) > 1 + len(one_way):
         tables, _ = best_of(lines[1 + len(one_way) :], 0, tables)
     table = tables[0]

time: 25.8 us -> 25.5 us (0.988)
  Pallas kernels: 2.78 us -> 2.27 us
    pallas_call x3 -> x2, Pallas kernels: 1.57 us -> 1.06 us  [best_of(): pl.pallas_call(lambda *refs: best_kernel(len(lines), back_count, len(tabl...]
  transfers between devices with their start and end apart: 8 -> 8, of which waited for: 3 -> 4; matrix products, arithmetic and copies ran while one was open for 0% -> 0% of each run, Pallas kernels for 9% -> 7%
where the time goes in v6:
time: 25.5 us; the launch traced here: 25.4 us
  starting transfers between devices  11.8 us (46%)
  waiting for transfers between devices  9.75 us (38%)
  Pallas kernels  2.27 us (9%)
  local copies, waits for them, and re-layouts  1.02 us (4%)
  other arithmetic  0.52 us (2%)
    ppermute x8, starting transfers between devices, shifted(): return lax.ppermute(value, axis, pairs)  11.8 us
    ppermute x8, waiting for transfers between devices, shifted(): return lax.ppermute(value, axis, pairs)  9.75 us
    pallas_call x1, Pallas kernels, body(): pl.pallas_call(stage_kernel, out_shape=[jax.ShapeDtypeStruct(message.shap...  1.16 us
    pallas_call x2, Pallas kernels, best_of(): pl.pallas_call(lambda *refs: best_kernel(len(lines), back_count, len(tabl...  1.06 us
    unnamed x6, local copies, waits for them, and re-layouts  0.97 us
    reshape x1, other arithmetic, body(): return nearest.reshape(row_count)  0.52 us
  transfers between devices with their start and end apart: 8, of which 4 were waited for; matrix products, arithmetic and copies ran while one was open for 0% of the time, Pallas kernels for 7%

profile of v6, /device:TPU:0, one launch (start us, length us, event | category | flops | bytes accessed | tf_op | source)
XLA Modules:
  0.0 25.4 jit_solution(16737236133462367193)
XLA Ops:
  0.0 0.0 copy-start
  0.0 0.0 copy-start.1
  0.0 0.0 copy-start.2
  0.0 0.7 %copy-done.1 = s32[128]{0:T(128)S(1)} copy-done((s32[128]{0:T(128)S(1)}, s32[128]{0:T(128)}, u32[]{:S(2)}) %copy-start.1) | copy-done | bytes 536
  0.7 0.0 copy-done.2
  0.7 0.3 copy-done
  1.1 4.1 %collective-permute-start.4 = (bf16[1040,128]{1,0:T(8,128)(2,1)S(1)}, bf16[1040,128]{1,0:T(8,128)(2,1)S(1)}, u32[]{:S(2)}, u32[]{:S(2)}) collective-permute-start(bf16[1040,128]{1,0:T(8,128)(2,1)S(1)} %pack.1.refs_1_.refs_2_), channel_id=1, source_target_pairs={{0,8},{8,4},{4,12},{12,0},{1,9},{9,5},{5,13},{13,1},{2,10},{10,6},... | collective-permute-start | bytes 798728 | tf_op jit(solution)/shard_map/ppermute | solution.py:104
  5.2 1.6 %collective-permute-start.3 = (bf16[1040,128]{1,0:T(8,128)(2,1)S(1)}, bf16[1040,128]{1,0:T(8,128)(2,1)S(1)}, u32[]{:S(2)}, u32[]{:S(2)}) collective-permute-start(bf16[1040,128]{1,0:T(8,128)(2,1)S(1)} %pack.1.refs_1_.refs_2_), channel_id=1, source_target_pairs={{0,4},{8,12},{4,0},{12,8},{1,5},{9,13},{5,1},{13,9},{2,6},{10,14},... | collective-permute-start | bytes 798728 | tf_op jit(solution)/shard_map/ppermute | solution.py:104
  6.7 9.6 %conditional.1 = (bf16[1040,128]{1,0:T(8,128)(2,1)}, bf16[1040,128]{1,0:T(8,128)(2,1)}, bf16[1040,128]{1,0:T(8,128)(2,1)}) conditional(s32[]{:T(128)} %convert_element_type.3, () %tuple.15, bf16[1040,128]{1,0:T(8,128)(2,1)S(1)} %pack.1.refs_1_.refs_2_), branch_computations={%region_0.0_spmd, %region_1.0_spmd} | conditional | bytes 3195024 | solution.py:142
  6.7 1.5 %collective-permute-start.1 = (bf16[1040,128]{1,0:T(8,128)(2,1)S(1)}, bf16[1040,128]{1,0:T(8,128)(2,1)}, u32[]{:S(2)}, u32[]{:S(2)}) collective-permute-start(bf16[1040,128]{1,0:T(8,128)(2,1)S(1)} %param.1), channel_id=1, source_target_pairs={{0,2},{2,0},{1,3},{3,1},{4,6},{6,4},{5,7},{7,5},{8,10},{10,8},{9,1... | collective-permute-start | bytes 798728 | tf_op jit(solution)/shard_map/cond/branch_1_fun/ppermute | solution.py:104
  8.2 0.0 collective-permute-start
  8.2 6.2 %collective-permute-done.1 = bf16[1040,128]{1,0:T(8,128)(2,1)} collective-permute-done((bf16[1040,128]{1,0:T(8,128)(2,1)S(1)}, bf16[1040,128]{1,0:T(8,128)(2,1)}, u32[]{:S(2)}, u32[]{:S(2)}) %collective-permute-start.1) | collective-permute-done | bytes 266272 | tf_op jit(solution)/shard_map/cond/branch_1_fun/ppermute | solution.py:104
  14.4 0.0 collective-permute-start.2
  14.4 0.0 collective-permute-done
  14.4 1.9 %collective-permute-done.2 = bf16[1040,128]{1,0:T(8,128)(2,1)} collective-permute-done((bf16[1040,128]{1,0:T(8,128)(2,1)}, bf16[1040,128]{1,0:T(8,128)(2,1)}, u32[]{:S(2)}, u32[]{:S(2)}) %collective-permute-start.2) | collective-permute-done | bytes 266272 | tf_op jit(solution)/shard_map/cond/branch_1_fun/ppermute | solution.py:104
  16.3 1.2 %stage.1 = (bf16[1040,128]{1,0:T(8,128)(2,1)S(1)}, bf16[1040,128]{1,0:T(8,128)(2,1)S(1)}, bf16[1040,128]{1,0:T(8,128)(2,1)S(1)}) custom-call(bf16[1040,128]{1,0:T(8,128)(2,1)} %get-tuple-element.21.refs_0_, bf16[1040,128]{1,0:T(8,128)(2,1)} %get-tuple-element.22.refs_1_, bf16[1040,128]{1,0:T(8,128)(2,1)} %get-tuple-element.23.refs_2_), custom_call_target="tpu_custom_call" | custom-call | tf_op jit(solution)/shard_map/stage/pallas_call | solution.py:148
  17.5 0.0 collective-permute-done.4.refs_0_
  17.5 0.6 %best.2 = (f32[2,128]{1,0:T(2,128)S(1)}, f32[2,128]{1,0:T(2,128)S(1)}, f32[1,128]{1,0:T(1,128)S(1)}) custom-call(bf16[1040,128]{1,0:T(8,128)(2,1)S(1)} %collective-permute-done.4.refs_0_, bf16[1040,128]{1,0:T(8,128)(2,1)S(1)} %pack.1.refs_1_.refs_2_, bf16[1040,128]{1,0:T(8,128)(2,1)S(1)} %pack.1.refs_1_.refs_2_, ...), custom_call_target="tpu_custom_call" | custom-call | tf_op jit(solution)/shard_map/best/pallas_call | solution.py:160
  18.0 0.3 %collective-permute-done.3.refs_0_ = bf16[1040,128]{1,0:T(8,128)(2,1)S(1)} collective-permute-done((bf16[1040,128]{1,0:T(8,128)(2,1)S(1)}, bf16[1040,128]{1,0:T(8,128)(2,1)S(1)}, u32[]{:S(2)}, u32[]{:S(2)}) %collective-permute-start.3) | collective-permute-done | bytes 266272 | tf_op jit(solution)/shard_map/ppermute | solution.py:104
  18.4 0.5 %best.3 = (f32[2,128]{1,0:T(2,128)S(1)}, f32[2,128]{1,0:T(2,128)S(1)}) custom-call(bf16[1040,128]{1,0:T(8,128)(2,1)S(1)} %collective-permute-done.3.refs_0_, bf16[1040,128]{1,0:T(8,128)(2,1)S(1)} %pack.1.refs_1_.refs_2_, bf16[1040,128]{1,0:T(8,128)(2,1)S(1)} %get-tuple-element.24.refs_3_.refs_2_, bf16[1040,128]{1,0:T(8,128)(2,1)S(1)} %get-tuple-element.25.refs_4_.refs_3_, ...), custom_call_target="tpu_custom_call" | custom-call | tf_op jit(solution)/shard_map/best/pallas_call | solution.py:160
  18.9 1.6 %collective-permute-start.5 = (f32[2,128]{1,0:T(2,128)S(1)}, f32[2,128]{1,0:T(2,128)S(1)}, u32[]{:S(2)}, u32[]{:S(2)}) collective-permute-start(f32[2,128]{1,0:T(2,128)S(1)} %get-tuple-element.30), channel_id=1, source_target_pairs={{0,2},{2,0},{1,3},{3,1},{4,6},{6,4},{5,7},{7,5},{8,10},{10,8},{9,1... | collective-permute-start | bytes 3080 | tf_op jit(solution)/shard_map/ppermute | solution.py:104
  20.4 3.0 %collective-permute-start.7 = (f32[1,128]{1,0:T(1,128)S(1)}, f32[1,128]{1,0:T(1,128)S(1)}, u32[]{:S(2)}, u32[]{:S(2)}) collective-permute-start(f32[1,128]{1,0:T(1,128)S(1)} %get-tuple-element.31), channel_id=1, source_target_pairs={{0,12},{8,0},{4,8},{12,4},{1,13},{9,1},{5,9},{13,5},{2,14},{10,2},... | collective-permute-start | bytes 1544 | tf_op jit(solution)/shard_map/ppermute | solution.py:104
  23.4 0.0 collective-permute-done.5
  23.5 0.1 collective-permute-start.6
  23.5 1.3 %collective-permute-done.7 = f32[1,128]{1,0:T(1,128)S(1)} collective-permute-done((f32[1,128]{1,0:T(1,128)S(1)}, f32[1,128]{1,0:T(1,128)S(1)}, u32[]{:S(2)}, u32[]{:S(2)}) %collective-permute-start.7) | collective-permute-done | bytes 544 | tf_op jit(solution)/shard_map/ppermute | solution.py:104
  24.9 0.0 collective-permute-done.6
  24.9 0.5 %maximum_bitcast_fusion = f32[128]{0:T(128)} fusion(f32[1,128]{1,0:T(1,128)S(1)} %collective-permute-done.7, f32[1,128]{1,0:T(1,128)S(1)} %collective-permute-done.6, f32[2,128]{1,0:T(2,128)S(1)} %max.9), kind=kLoop, calls=%fused_computation.1 | loop fusion | flops 256 | bytes 2048 | tf_op jit(solution)/shard_map/reshape | solution.py:186
  (5 shorter events, 0.1 us)
Async XLA Ops:
  0.0 1.0 %copy-start = (bf16[128,1024]{1,0:T(8,128)(2,1)S(1)}, bf16[128,1024]{1,0:T(8,128)(2,1)}, u32[]{:S(2)}) copy-start(bf16[128,1024]{1,0:T(8,128)(2,1)} %param.5) | copy-start | bytes 786436
  0.0 0.7 %copy-start.1 = (s32[128]{0:T(128)S(1)}, s32[128]{0:T(128)}, u32[]{:S(2)}) copy-start(s32[128]{0:T(128)} %param.6) | copy-start | bytes 1540
  0.0 0.7 %copy-start.2 = (s32[128]{0:T(128)S(1)}, s32[128]{0:T(128)}, u32[]{:S(2)}) copy-start(s32[128]{0:T(128)} %param.7) | copy-start | bytes 1540
  1.1 16.4 %collective-permute-start.4 = (bf16[1040,128]{1,0:T(8,128)(2,1)S(1)}, bf16[1040,128]{1,0:T(8,128)(2,1)S(1)}, u32[]{:S(2)}, u32[]{:S(2)}) collective-permute-start(bf16[1040,128]{1,0:T(8,128)(2,1)S(1)} %pack.1.refs_1_.refs_2_), channel_id=1, source_target_pairs={{0,8},{8,4},{4,12},{12,0},{1,9},{9,5},{5,13},{13,1},{2,10},{10,6},... | collective-permute-start | bytes 798728 | tf_op jit(solution)/shard_map/ppermute | solution.py:104
  5.2 13.2 %collective-permute-start.3 = (bf16[1040,128]{1,0:T(8,128)(2,1)S(1)}, bf16[1040,128]{1,0:T(8,128)(2,1)S(1)}, u32[]{:S(2)}, u32[]{:S(2)}) collective-permute-start(bf16[1040,128]{1,0:T(8,128)(2,1)S(1)} %pack.1.refs_1_.refs_2_), channel_id=1, source_target_pairs={{0,4},{8,12},{4,0},{12,8},{1,5},{9,13},{5,1},{13,9},{2,6},{10,14},... | collective-permute-start | bytes 798728 | tf_op jit(solution)/shard_map/ppermute | solution.py:104
  6.7 7.7 %collective-permute-start.1 = (bf16[1040,128]{1,0:T(8,128)(2,1)S(1)}, bf16[1040,128]{1,0:T(8,128)(2,1)}, u32[]{:S(2)}, u32[]{:S(2)}) collective-permute-start(bf16[1040,128]{1,0:T(8,128)(2,1)S(1)} %param.1), channel_id=1, source_target_pairs={{0,2},{2,0},{1,3},{3,1},{4,6},{6,4},{5,7},{7,5},{8,10},{10,8},{9,1... | collective-permute-start | bytes 798728 | tf_op jit(solution)/shard_map/cond/branch_1_fun/ppermute | solution.py:104
  8.2 6.2 %collective-permute-start = (bf16[1040,128]{1,0:T(8,128)(2,1)S(1)}, bf16[1040,128]{1,0:T(8,128)(2,1)}, u32[]{:S(2)}, u32[]{:S(2)}) collective-permute-start(bf16[1040,128]{1,0:T(8,128)(2,1)S(1)} %param.1), channel_id=1, source_target_pairs={{0,1},{1,0},{2,3},{3,2},{4,5},{5,4},{6,7},{7,6},{8,9},{9,8},{10,11... | collective-permute-start | bytes 798728 | tf_op jit(solution)/shard_map/cond/branch_1_fun/ppermute | solution.py:104
  14.4 1.9 %collective-permute-start.2 = (bf16[1040,128]{1,0:T(8,128)(2,1)}, bf16[1040,128]{1,0:T(8,128)(2,1)}, u32[]{:S(2)}, u32[]{:S(2)}) collective-permute-start(bf16[1040,128]{1,0:T(8,128)(2,1)} %collective-permute-done.1), channel_id=1, source_target_pairs={{0,1},{1,0},{2,3},{3,2},{4,5},{5,4},{6,7},{7,6},{8,9},{9,8},{10,11... | collective-permute-start | bytes 798728 | tf_op jit(solution)/shard_map/cond/branch_1_fun/ppermute | solution.py:104
  18.9 4.6 %collective-permute-start.5 = (f32[2,128]{1,0:T(2,128)S(1)}, f32[2,128]{1,0:T(2,128)S(1)}, u32[]{:S(2)}, u32[]{:S(2)}) collective-permute-start(f32[2,128]{1,0:T(2,128)S(1)} %get-tuple-element.30), channel_id=1, source_target_pairs={{0,2},{2,0},{1,3},{3,1},{4,6},{6,4},{5,7},{7,5},{8,10},{10,8},{9,1... | collective-permute-start | bytes 3080 | tf_op jit(solution)/shard_map/ppermute | solution.py:104
  20.4 4.4 %collective-permute-start.7 = (f32[1,128]{1,0:T(1,128)S(1)}, f32[1,128]{1,0:T(1,128)S(1)}, u32[]{:S(2)}, u32[]{:S(2)}) collective-permute-start(f32[1,128]{1,0:T(1,128)S(1)} %get-tuple-element.31), channel_id=1, source_target_pairs={{0,12},{8,0},{4,8},{12,4},{1,13},{9,1},{5,9},{13,5},{2,14},{10,2},... | collective-permute-start | bytes 1544 | tf_op jit(solution)/shard_map/ppermute | solution.py:104
  23.5 1.4 %collective-permute-start.6 = (f32[1,128]{1,0:T(1,128)S(1)}, f32[1,128]{1,0:T(1,128)S(1)}, u32[]{:S(2)}, u32[]{:S(2)}) collective-permute-start(f32[1,128]{1,0:T(1,128)S(1)} %slice.7), channel_id=1, source_target_pairs={{0,1},{1,0},{2,3},{3,2},{4,5},{5,4},{6,7},{7,6},{8,9},{9,8},{10,11... | collective-permute-start | bytes 1544 | tf_op jit(solution)/shard_map/ppermute | solution.py:104

commit v7 on v6

--- a/solution.py
+++ b/solution.py
@@ -31,12 +31,6 @@
     copy.wait()
 
 
-def stage_kernel(*refs):
-    half = len(refs) // 2
-    for source, target in zip(refs[:half], refs[half:]):
-        target[...] = source[...]
-
-
 def rows_of(message):
     rows = message.shape[1]
     chunks = message.shape[0] // rows
@@ -48,16 +42,24 @@
     return meta[0:1], meta[1:2] * DIGIT + meta[2:3]
 
 
+def stage_kernel(*refs):
+    blocks, (rows_ref, meta_ref) = refs[:-2], refs[-2:]
+    for index, block in enumerate(blocks):
+        rows = block.shape[1]
+        rows_ref[index * rows : (index + 1) * rows, :] = rows_of(block)
+        meta_ref[:, index * rows : (index + 1) * rows] = block[block.shape[0] - META_ROWS :, :]
+
+
 def best_kernel(line_count, back_count, table_count, mem_count, sub_count, *refs):
     plane_count = mem_count * sub_count
     lines, refs = refs[:line_count], refs[line_count:]
-    plane, refs = refs[:plane_count], refs[plane_count:]
+    plane, plane_meta, refs = refs[0], refs[1], refs[2:]
     tables, outs = refs[:table_count], refs[table_count:]
     plane_outs, back_outs = outs[:mem_count], outs[mem_count:]
     rows = lines[0].shape[1]
 
     line_rows = jnp.concatenate([rows_of(line) for line in lines], axis=0)
-    plane_rows = jnp.concatenate([rows_of(block) for block in plane], axis=0)
+    plane_rows = plane[...]
     metas = [part for line in lines for part in meta_of(line)]
     metas += [metas[-1]] * (-len(metas) % SUBLANES)
     columns = jnp.transpose(jnp.concatenate(metas, axis=0))
@@ -68,7 +70,7 @@
         )
         for part in range(2)
     ]
-    label, rank = [jnp.concatenate(parts, axis=1) for parts in zip(*map(meta_of, plane))]
+    label, rank = meta_of(plane_meta)
 
     scores = lax.dot_general(line_rows, plane_rows, NT, preferred_element_type=jnp.float32)
     scores = jnp.where(line_label == label, scores, NONE)
@@ -145,15 +147,18 @@
         lambda block: [jnp.zeros_like(block)] * (sub_count * mem_count - 1),
         message,
     )
-    near = pl.pallas_call(
+    plane_width = row_count * mem_count * sub_count
+    plane = pl.pallas_call(
         stage_kernel,
-        out_shape=[jax.ShapeDtypeStruct(message.shape, message.dtype)] * len(near),
-        in_specs=[vmem] * len(near),
-        out_specs=[vmem] * len(near),
+        out_shape=[
+            jax.ShapeDtypeStruct((plane_width, feature_count), jnp.bfloat16),
+            jax.ShapeDtypeStruct((META_ROWS, plane_width), jnp.bfloat16),
+        ],
+        in_specs=[vmem] * (1 + len(near)),
+        out_specs=[vmem, vmem],
         compiler_params=params,
         name="stage",
-    )(*near)
-    plane = [message, *near]
+    )(message, *near)
 
     def best_of(lines, back_count, tables):
         operands = [*lines, *plane, *tables]

time: 25.5 us -> 25.5 us (level)
  no operation moved by 1% of the time
where the time goes in v7:
time: 25.5 us; the launch traced here: 25.4 us
  starting transfers between devices  11.8 us (46%)
  waiting for transfers between devices  9.68 us (38%)
  Pallas kernels  2.34 us (9%)
  local copies, waits for them, and re-layouts  1.02 us (4%)
  other arithmetic  0.52 us (2%)
    ppermute x8, starting transfers between devices, shifted(): return lax.ppermute(value, axis, pairs)  11.8 us
    ppermute x8, waiting for transfers between devices, shifted(): return lax.ppermute(value, axis, pairs)  9.68 us
    pallas_call x1, Pallas kernels, body(): pl.pallas_call(stage_kernel, out_shape=[jax.ShapeDtypeStruct((plane_width...  1.24 us
    pallas_call x2, Pallas kernels, best_of(): pl.pallas_call(lambda *refs: best_kernel(len(lines), back_count, len(tabl...  1.06 us
    unnamed x6, local copies, waits for them, and re-layouts  0.97 us
    reshape x1, other arithmetic, body(): return nearest.reshape(row_count)  0.52 us
  transfers between devices with their start and end apart: 8, of which 4 were waited for; matrix products, arithmetic and copies ran while one was open for 0% of the time, Pallas kernels for 7%

profile of v7, /device:TPU:0, one launch (start us, length us, event | category | flops | bytes accessed | tf_op | source)
XLA Modules:
  0.0 25.4 jit_solution(300307925960878532)
XLA Ops:
  0.0 0.0 copy-start
  0.0 0.0 copy-start.1
  0.0 0.0 copy-start.2
  0.0 0.7 %copy-done.1 = s32[128]{0:T(128)S(1)} copy-done((s32[128]{0:T(128)S(1)}, s32[128]{0:T(128)}, u32[]{:S(2)}) %copy-start.1) | copy-done | bytes 536
  0.7 0.0 copy-done.2
  0.7 0.3 copy-done
  1.1 4.1 %collective-permute-start.4 = (bf16[1040,128]{1,0:T(8,128)(2,1)S(1)}, bf16[1040,128]{1,0:T(8,128)(2,1)S(1)}, u32[]{:S(2)}, u32[]{:S(2)}) collective-permute-start(bf16[1040,128]{1,0:T(8,128)(2,1)S(1)} %pack.1.refs_0_.refs_1_), channel_id=1, source_target_pairs={{0,8},{8,4},{4,12},{12,0},{1,9},{9,5},{5,13},{13,1},{2,10},{10,6},... | collective-permute-start | bytes 798728 | tf_op jit(solution)/shard_map/ppermute | solution.py:106
  5.2 1.6 %collective-permute-start.3 = (bf16[1040,128]{1,0:T(8,128)(2,1)S(1)}, bf16[1040,128]{1,0:T(8,128)(2,1)S(1)}, u32[]{:S(2)}, u32[]{:S(2)}) collective-permute-start(bf16[1040,128]{1,0:T(8,128)(2,1)S(1)} %pack.1.refs_0_.refs_1_), channel_id=1, source_target_pairs={{0,4},{8,12},{4,0},{12,8},{1,5},{9,13},{5,1},{13,9},{2,6},{10,14},... | collective-permute-start | bytes 798728 | tf_op jit(solution)/shard_map/ppermute | solution.py:106
  6.7 9.6 %conditional.1 = (bf16[1040,128]{1,0:T(8,128)(2,1)}, bf16[1040,128]{1,0:T(8,128)(2,1)}, bf16[1040,128]{1,0:T(8,128)(2,1)}) conditional(s32[]{:T(128)} %convert_element_type.3, () %tuple.15, bf16[1040,128]{1,0:T(8,128)(2,1)S(1)} %pack.1.refs_0_.refs_1_), branch_computations={%region_0.0_spmd, %region_1.0_spmd} | conditional | bytes 3195024 | solution.py:144
  6.7 1.5 %collective-permute-start.1 = (bf16[1040,128]{1,0:T(8,128)(2,1)S(1)}, bf16[1040,128]{1,0:T(8,128)(2,1)}, u32[]{:S(2)}, u32[]{:S(2)}) collective-permute-start(bf16[1040,128]{1,0:T(8,128)(2,1)S(1)} %param.1), channel_id=1, source_target_pairs={{0,2},{2,0},{1,3},{3,1},{4,6},{6,4},{5,7},{7,5},{8,10},{10,8},{9,1... | collective-permute-start | bytes 798728 | tf_op jit(solution)/shard_map/cond/branch_1_fun/ppermute | solution.py:106
  8.2 0.0 collective-permute-start
  8.2 6.2 %collective-permute-done.1 = bf16[1040,128]{1,0:T(8,128)(2,1)} collective-permute-done((bf16[1040,128]{1,0:T(8,128)(2,1)S(1)}, bf16[1040,128]{1,0:T(8,128)(2,1)}, u32[]{:S(2)}, u32[]{:S(2)}) %collective-permute-start.1) | collective-permute-done | bytes 266272 | tf_op jit(solution)/shard_map/cond/branch_1_fun/ppermute | solution.py:106
  14.4 0.0 collective-permute-start.2
  14.4 0.0 collective-permute-done
  14.4 1.9 %collective-permute-done.2 = bf16[1040,128]{1,0:T(8,128)(2,1)} collective-permute-done((bf16[1040,128]{1,0:T(8,128)(2,1)}, bf16[1040,128]{1,0:T(8,128)(2,1)}, u32[]{:S(2)}, u32[]{:S(2)}) %collective-permute-start.2) | collective-permute-done | bytes 266272 | tf_op jit(solution)/shard_map/cond/branch_1_fun/ppermute | solution.py:106
  16.3 1.2 %stage.1 = (bf16[512,1024]{1,0:T(8,128)(2,1)S(1)}, bf16[16,512]{1,0:T(8,128)(2,1)S(1)}) custom-call(bf16[1040,128]{1,0:T(8,128)(2,1)S(1)} %pack.1.refs_0_.refs_1_, bf16[1040,128]{1,0:T(8,128)(2,1)} %get-tuple-element.20.refs_1_, bf16[1040,128]{1,0:T(8,128)(2,1)} %get-tuple-element.21.refs_2_, bf16[1040,128]{1,0:T(8,128)(2,1)} %get-tuple-element.22.refs_3_), custom_call_target="tpu_custom_call" | custom-call | tf_op jit(solution)/shard_map/stage/pallas_call | solution.py:151
  17.5 0.0 collective-permute-done.4.refs_0_
  17.6 0.6 %best.2 = (f32[2,128]{1,0:T(2,128)S(1)}, f32[2,128]{1,0:T(2,128)S(1)}, f32[1,128]{1,0:T(1,128)S(1)}) custom-call(bf16[1040,128]{1,0:T(8,128)(2,1)S(1)} %collective-permute-done.4.refs_0_, bf16[1040,128]{1,0:T(8,128)(2,1)S(1)} %pack.1.refs_0_.refs_1_, bf16[512,1024]{1,0:T(8,128)(2,1)S(1)} %get-tuple-element.23.refs_2_.refs_1_, ...), custom_call_target="tpu_custom_call" | custom-call | tf_op jit(solution)/shard_map/best/pallas_call | solution.py:165
  18.1 0.3 %collective-permute-done.3.refs_0_ = bf16[1040,128]{1,0:T(8,128)(2,1)S(1)} collective-permute-done((bf16[1040,128]{1,0:T(8,128)(2,1)S(1)}, bf16[1040,128]{1,0:T(8,128)(2,1)S(1)}, u32[]{:S(2)}, u32[]{:S(2)}) %collective-permute-start.3) | collective-permute-done | bytes 266272 | tf_op jit(solution)/shard_map/ppermute | solution.py:106
  18.4 0.5 %best.3 = (f32[2,128]{1,0:T(2,128)S(1)}, f32[2,128]{1,0:T(2,128)S(1)}) custom-call(bf16[1040,128]{1,0:T(8,128)(2,1)S(1)} %collective-permute-done.3.refs_0_, bf16[512,1024]{1,0:T(8,128)(2,1)S(1)} %get-tuple-element.23.refs_2_.refs_1_, bf16[16,512]{1,0:T(8,128)(2,1)S(1)} %get-tuple-element.24.refs_3_.refs_2_, f32[2,128]{1,0:T(2,128)S(1)} %get-tuple-element.25.refs_3_, ...), custom_call_target="tpu_custom_call" | custom-call | tf_op jit(solution)/shard_map/best/pallas_call | solution.py:165
  18.9 1.6 %collective-permute-start.5 = (f32[2,128]{1,0:T(2,128)S(1)}, f32[2,128]{1,0:T(2,128)S(1)}, u32[]{:S(2)}, u32[]{:S(2)}) collective-permute-start(f32[2,128]{1,0:T(2,128)S(1)} %get-tuple-element.28), channel_id=1, source_target_pairs={{0,2},{2,0},{1,3},{3,1},{4,6},{6,4},{5,7},{7,5},{8,10},{10,8},{9,1... | collective-permute-start | bytes 3080 | tf_op jit(solution)/shard_map/ppermute | solution.py:106
  20.4 3.0 %collective-permute-start.7 = (f32[1,128]{1,0:T(1,128)S(1)}, f32[1,128]{1,0:T(1,128)S(1)}, u32[]{:S(2)}, u32[]{:S(2)}) collective-permute-start(f32[1,128]{1,0:T(1,128)S(1)} %get-tuple-element.29), channel_id=1, source_target_pairs={{0,12},{8,0},{4,8},{12,4},{1,13},{9,1},{5,9},{13,5},{2,14},{10,2},... | collective-permute-start | bytes 1544 | tf_op jit(solution)/shard_map/ppermute | solution.py:106
  23.4 0.0 collective-permute-done.5
  23.4 0.1 collective-permute-start.6
  23.5 1.4 %collective-permute-done.7 = f32[1,128]{1,0:T(1,128)S(1)} collective-permute-done((f32[1,128]{1,0:T(1,128)S(1)}, f32[1,128]{1,0:T(1,128)S(1)}, u32[]{:S(2)}, u32[]{:S(2)}) %collective-permute-start.7) | collective-permute-done | bytes 544 | tf_op jit(solution)/shard_map/ppermute | solution.py:106
  24.9 0.0 collective-permute-done.6
  24.9 0.5 %maximum_bitcast_fusion = f32[128]{0:T(128)} fusion(f32[1,128]{1,0:T(1,128)S(1)} %collective-permute-done.7, f32[1,128]{1,0:T(1,128)S(1)} %collective-permute-done.6, f32[2,128]{1,0:T(2,128)S(1)} %max.9), kind=kLoop, calls=%fused_computation.1 | loop fusion | flops 256 | bytes 2048 | tf_op jit(solution)/shard_map/reshape | solution.py:191
  (5 shorter events, 0.1 us)
Async XLA Ops:
  0.0 1.0 %copy-start = (bf16[128,1024]{1,0:T(8,128)(2,1)S(1)}, bf16[128,1024]{1,0:T(8,128)(2,1)}, u32[]{:S(2)}) copy-start(bf16[128,1024]{1,0:T(8,128)(2,1)} %param.5) | copy-start | bytes 786436
  0.0 0.7 %copy-start.1 = (s32[128]{0:T(128)S(1)}, s32[128]{0:T(128)}, u32[]{:S(2)}) copy-start(s32[128]{0:T(128)} %param.6) | copy-start | bytes 1540
  0.0 0.7 %copy-start.2 = (s32[128]{0:T(128)S(1)}, s32[128]{0:T(128)}, u32[]{:S(2)}) copy-start(s32[128]{0:T(128)} %param.7) | copy-start | bytes 1540
  1.1 16.5 %collective-permute-start.4 = (bf16[1040,128]{1,0:T(8,128)(2,1)S(1)}, bf16[1040,128]{1,0:T(8,128)(2,1)S(1)}, u32[]{:S(2)}, u32[]{:S(2)}) collective-permute-start(bf16[1040,128]{1,0:T(8,128)(2,1)S(1)} %pack.1.refs_0_.refs_1_), channel_id=1, source_target_pairs={{0,8},{8,4},{4,12},{12,0},{1,9},{9,5},{5,13},{13,1},{2,10},{10,6},... | collective-permute-start | bytes 798728 | tf_op jit(solution)/shard_map/ppermute | solution.py:106
  5.2 13.2 %collective-permute-start.3 = (bf16[1040,128]{1,0:T(8,128)(2,1)S(1)}, bf16[1040,128]{1,0:T(8,128)(2,1)S(1)}, u32[]{:S(2)}, u32[]{:S(2)}) collective-permute-start(bf16[1040,128]{1,0:T(8,128)(2,1)S(1)} %pack.1.refs_0_.refs_1_), channel_id=1, source_target_pairs={{0,4},{8,12},{4,0},{12,8},{1,5},{9,13},{5,1},{13,9},{2,6},{10,14},... | collective-permute-start | bytes 798728 | tf_op jit(solution)/shard_map/ppermute | solution.py:106
  6.7 7.7 %collective-permute-start.1 = (bf16[1040,128]{1,0:T(8,128)(2,1)S(1)}, bf16[1040,128]{1,0:T(8,128)(2,1)}, u32[]{:S(2)}, u32[]{:S(2)}) collective-permute-start(bf16[1040,128]{1,0:T(8,128)(2,1)S(1)} %param.1), channel_id=1, source_target_pairs={{0,2},{2,0},{1,3},{3,1},{4,6},{6,4},{5,7},{7,5},{8,10},{10,8},{9,1... | collective-permute-start | bytes 798728 | tf_op jit(solution)/shard_map/cond/branch_1_fun/ppermute | solution.py:106
  8.2 6.2 %collective-permute-start = (bf16[1040,128]{1,0:T(8,128)(2,1)S(1)}, bf16[1040,128]{1,0:T(8,128)(2,1)}, u32[]{:S(2)}, u32[]{:S(2)}) collective-permute-start(bf16[1040,128]{1,0:T(8,128)(2,1)S(1)} %param.1), channel_id=1, source_target_pairs={{0,1},{1,0},{2,3},{3,2},{4,5},{5,4},{6,7},{7,6},{8,9},{9,8},{10,11... | collective-permute-start | bytes 798728 | tf_op jit(solution)/shard_map/cond/branch_1_fun/ppermute | solution.py:106
  14.4 1.9 %collective-permute-start.2 = (bf16[1040,128]{1,0:T(8,128)(2,1)}, bf16[1040,128]{1,0:T(8,128)(2,1)}, u32[]{:S(2)}, u32[]{:S(2)}) collective-permute-start(bf16[1040,128]{1,0:T(8,128)(2,1)} %collective-permute-done.1), channel_id=1, source_target_pairs={{0,1},{1,0},{2,3},{3,2},{4,5},{5,4},{6,7},{7,6},{8,9},{9,8},{10,11... | collective-permute-start | bytes 798728 | tf_op jit(solution)/shard_map/cond/branch_1_fun/ppermute | solution.py:106
  18.9 4.6 %collective-permute-start.5 = (f32[2,128]{1,0:T(2,128)S(1)}, f32[2,128]{1,0:T(2,128)S(1)}, u32[]{:S(2)}, u32[]{:S(2)}) collective-permute-start(f32[2,128]{1,0:T(2,128)S(1)} %get-tuple-element.28), channel_id=1, source_target_pairs={{0,2},{2,0},{1,3},{3,1},{4,6},{6,4},{5,7},{7,5},{8,10},{10,8},{9,1... | collective-permute-start | bytes 3080 | tf_op jit(solution)/shard_map/ppermute | solution.py:106
  20.4 4.4 %collective-permute-start.7 = (f32[1,128]{1,0:T(1,128)S(1)}, f32[1,128]{1,0:T(1,128)S(1)}, u32[]{:S(2)}, u32[]{:S(2)}) collective-permute-start(f32[1,128]{1,0:T(1,128)S(1)} %get-tuple-element.29), channel_id=1, source_target_pairs={{0,12},{8,0},{4,8},{12,4},{1,13},{9,1},{5,9},{13,5},{2,14},{10,2},... | collective-permute-start | bytes 1544 | tf_op jit(solution)/shard_map/ppermute | solution.py:106
  23.4 1.4 %collective-permute-start.6 = (f32[1,128]{1,0:T(1,128)S(1)}, f32[1,128]{1,0:T(1,128)S(1)}, u32[]{:S(2)}, u32[]{:S(2)}) collective-permute-start(f32[1,128]{1,0:T(1,128)S(1)} %slice.7), channel_id=1, source_target_pairs={{0,1},{1,0},{2,3},{3,2},{4,5},{5,4},{6,7},{7,6},{8,9},{9,8},{10,11... | collective-permute-start | bytes 1544 | tf_op jit(solution)/shard_map/ppermute | solution.py:106
